TPU v7x, 256 devices: a whole 4x4x8 slice. The times are simulated.
256 devices in a mesh: gx: 32 (over y, z), gy: 8 (over x, core).
Axes of the slice: x: 4, y: 4, z: 8, core: 2. Of those that a mesh axis runs over, the one named last changes fastest.
Arguments:
- tracer_cotangent: float32 [25, 512, 4096], P(None, 'gy', 'gx'), may hold values from -6 to 6
- height_cotangent: float32 [512, 4096], P('gy', 'gx'), may hold values from -6 to 6
- east_velocity: float32 [25, 512, 4096], P(None, 'gy', 'gx'), may hold values from -4 to 4
- north_velocity: float32 [25, 512, 4096], P(None, 'gy', 'gx'), may hold values from -4 to 4
- diffusivity: float32 [25, 512, 4096], P(None, 'gy', 'gx'), may hold values from 0.1 to 1
- thickness: float32 [25], replicated, may hold values from 0.5 to 2
- depth_levels: int32 [512, 4096], P('gy', 'gx'), may hold values from 0 to 25
- fold_partner: int32 [4096], P('gx'), may hold values from 0 to 4095, as said below
Outputs:
- tracer_adjoint: float32 [25, 512, 4096], P(None, 'gy', 'gx')
- height_adjoint: float32 [512, 4096], P('gy', 'gx')
Inputs may be any that keep to these rules, and one draw needn't show every extreme that they name: fold_partner[i] = (s - 1 - i) mod 4096 for one s, so the map is its own inverse.
All inputs are finite; a program needn't handle non-finite values.
Results may differ from a plain program's by a relative error of at most 0.00013.
Values sent between devices are 32-bit elements; how exact they have to be, the bound alone decides.
A program may use at most 128 MiB of HBM per device.

v0:
```python
import jax
import jax.numpy as jnp
from jax import lax
from jax.sharding import PartitionSpec as P

ITERS = 3


damping = 0.1
conduct = 1.0
time_step = 0.3


def with_halo(shard, sides, width):
    for axis, dim in sides:
        count, length = (lax.axis_size(axis), shard.shape[dim])
        up = [(i, (i + 1) % count) for i in range(count)]
        down = [(j, i) for i, j in up]
        last = lax.slice_in_dim(shard, length - width, length, axis=dim)
        initial = lax.slice_in_dim(shard, 0, width, axis=dim)
        before = lax.ppermute(last, axis, up)
        after = lax.ppermute(initial, axis, down)
        shard = jnp.concatenate([before, shard, after], axis=dim)
    return shard


def mirror_row(top_row, partner_local):
    whole_row = lax.all_gather(top_row, "gx", axis=1, tiled=True)
    return jnp.take(whole_row, partner_local, axis=1)


def extend_block(stack, signs, partner_local):
    padded = with_halo(stack, (("gx", 2), ("gy", 1)), 1)
    mirrored = mirror_row(stack[:, -1, :], partner_local) * signs[:, None]
    row_index = lax.axis_index("gy")
    north = jnp.where(row_index == lax.axis_size("gy") - 1, mirrored, padded[:, -1, 1:-1])
    south = jnp.where(row_index == 0, jnp.zeros_like(mirrored), padded[:, 0, 1:-1])
    return padded.at[:, -1, 1:-1].set(north).at[:, 0, 1:-1].set(south)


def sides(padded):
    return (
        padded[..., 1:-1, 2:],
        padded[..., 1:-1, :-2],
        padded[..., 2:, 1:-1],
        padded[..., :-2, 1:-1],
    )


def centre(padded):
    return padded[..., 1:-1, 1:-1]


def apply_operator(padded_field, conductances):
    middle = centre(padded_field)
    total = damping * middle
    for cond, nbr in zip(conductances, sides(padded_field)):
        total = total + cond * (middle - nbr)
    return total


def squares(residual):
    return lax.psum(jnp.sum(residual * residual), ("gx", "gy"))


def adjoint_levels(total, h_pad, w_pad, u_pad, v_pad, k_pad):
    h_c, w_c, u_c, v_c, k_c = (
        centre(h_pad),
        centre(w_pad),
        centre(u_pad),
        centre(v_pad),
        centre(k_pad),
    )
    h_e, h_w, h_n, h_s = sides(h_pad)
    w_e, w_w, w_n, w_s = sides(w_pad)
    u_e, u_w, u_n, u_s = sides(u_pad)
    v_e, v_w, v_n, v_s = sides(v_pad)
    k_e, k_w, k_n, k_s = sides(k_pad)
    east = (h_e - h_c) * w_c * w_e * ((u_c + u_e) * 0.25 + (k_c + k_e) * 0.5)
    west = (h_c - h_w) * w_w * w_c * ((u_w + u_c) * 0.25 - (k_w + k_c) * 0.5)
    north = (h_n - h_c) * w_c * w_n * ((v_c + v_n) * 0.25 + (k_c + k_n) * 0.5)
    south = (h_c - h_s) * w_s * w_c * ((v_s + v_c) * 0.25 - (k_s + k_c) * 0.5)
    return total + east + west + north + south


def local(
    tracer_cotangent,
    height_cotangent,
    east_velocity,
    north_velocity,
    diffusivity,
    thickness,
    depth_levels,
    fold_partner,
):
    nlevels = thickness.shape[0]
    levels_f = depth_levels.astype(jnp.float32)
    first = extend_block(
        jnp.stack([height_cotangent, levels_f]), jnp.ones((2,), jnp.float32), fold_partner
    )
    depth_pad = first[1]
    conductances = [conduct * jnp.minimum(levels_f, nbr) / nlevels for nbr in sides(depth_pad)]
    single = jnp.ones((1,), jnp.float32)
    height_adjoint = jnp.zeros_like(height_cotangent)
    residual = height_cotangent
    direction = residual
    padded_dir = first[0]
    norm_now = squares(residual)
    for step in range(ITERS):
        if step > 0:
            padded_dir = extend_block(direction[None], single, fold_partner)[0]
        image = apply_operator(padded_dir, conductances)
        alpha = norm_now / lax.psum(jnp.sum(direction * image), ("gx", "gy"))
        height_adjoint = height_adjoint + alpha * direction
        if step + 1 < ITERS:
            residual = residual - alpha * image
            norm_next = squares(residual)
            direction = residual + norm_next / norm_now * direction
            norm_now = norm_next
    level_ids = lax.broadcasted_iota(jnp.float32, (nlevels, 1, 1), 0)
    wet = (level_ids < levels_f[None]).astype(jnp.float32)
    total = tracer_cotangent + thickness[:, None, None] * wet * height_adjoint[None]
    scaled = time_step * wet * total
    stacked = jnp.concatenate([scaled, east_velocity, north_velocity, diffusivity], axis=0)
    ones_k = jnp.ones((nlevels,), jnp.float32)
    signs = jnp.concatenate([ones_k, ones_k, -ones_k, ones_k])
    padded = extend_block(stacked, signs, fold_partner)
    h_pad = padded[0:nlevels]
    u_pad = padded[nlevels : 2 * nlevels]
    v_pad = padded[2 * nlevels : 3 * nlevels]
    k_pad = padded[3 * nlevels :]
    w_pad = (level_ids < depth_pad[None]).astype(jnp.float32)
    tracer_adjoint = adjoint_levels(total, h_pad, w_pad, u_pad, v_pad, k_pad)
    return (tracer_adjoint, height_adjoint)


def solution(mesh):
    in_specs = (
        P(None, "gy", "gx"),
        P("gy", "gx"),
        P(None, "gy", "gx"),
        P(None, "gy", "gx"),
        P(None, "gy", "gx"),
        P(),
        P("gy", "gx"),
        P("gx"),
    )
    out_specs = (P(None, "gy", "gx"), P("gy", "gx"))
    return jax.shard_map(local, mesh=mesh, in_specs=in_specs, out_specs=out_specs, check_vma=False)
```

profile of v0, /device:TPU:1, one launch (start us, length us, event | category | flops | bytes accessed | tf_op | source)
XLA Modules:
  0.0 712.4 jit_solution(14432753816870265872)
XLA Ops:
  7.2 0.8 fusion.55
  8.0 0.9 fusion.26
  8.9 8.9 %collective-permute-start.1 = (f32[2,64,1]{2,1,0:T(8,128)S(1)}, f32[2,64,1]{2,1,0:T(8,128)S(1)}, u32[]{:S(2)}, u32[]{:S(2)}) collective-permute-start(f32[2,64,1]{2,1,0:T(8,128)S(1)} %get-tuple-element.138), channel_id=1, source_target_pairs={{8,0},{16,8},{24,16},{32,24},{40,32},{48,40},{56,48},{64,56},{72,6... | collective-permute-start | bytes 1544 | tf_op jit(solution)/shard_map/ppermute | solution.py:22
  17.8 0.7 compare_select_fusion
  18.5 0.7 compare_and_fusion
  19.2 0.6 fusion.58
  19.8 0.7 pad_maximum_fusion.20
  20.6 3.7 collective-permute-done
  24.3 0.9 pad_maximum_fusion.2
  25.3 2.1 collective-permute-start.3
  27.4 36.9 %all-gather = f32[2,1,4096]{0,2,1:T(8,128)S(1)} all-gather(f32[2,1,128]{0,2,1:T(8,128)S(1)} %copy.116), channel_id=2, replica_groups=mesh['gx'=32,'gy'=8] {'gx'}, dimensions={2}, use_global_device_ids=true | all-gather | bytes 33792 | tf_op jit(solution)/shard_map/all_gather | solution.py:28
  64.4 0.6 gather_fusion
  65.3 12.7 %collective-permute-start.2 = (f32[2,1,130]{1,2,0:T(8,128)S(1)}, f32[2,1,130]{1,2,0:T(8,128)S(1)}, u32[]{:S(2)}, u32[]{:S(2)}) collective-permute-start(f32[2,1,130]{1,2,0:T(8,128)S(1)} %copy.94), channel_id=1, source_target_pairs={{0,1},{1,2},{2,3},{3,4},{4,5},{5,6},{6,7},{7,0},{8,9},{9,10},{10,1... | collective-permute-start | bytes 3128 | tf_op jit(solution)/shard_map/ppermute | solution.py:21
  78.1 0.9 copy.99
  79.0 0.9 copy.97
  80.2 1.0 scatter.26
  81.2 1.9 scatter.29
  83.8 0.7 multiply_reduce_fusion.3
  84.5 76.1 %all-reduce = (f32[]{:T(128)}, f32[]{:T(128)}) all-reduce(f32[]{:T(128)} %get-tuple-element.112, f32[]{:T(128)} %get-tuple-element.111), channel_id=1, replica_groups=mesh['gx'=32,'gy'=8] {'gx','gy'}, use_global_device_ids=true, to_apply=%region_1.2 | all-reduce | flops 2 | bytes 16 | tf_op jit(solution)/shard_map/psum | solution.py:63
  162.0 0.6 multiply_reduce_fusion.2
  162.6 73.6 %psum.44 = f32[]{:T(128)} all-reduce(f32[]{:T(128)} %get-tuple-element.117), channel_id=1, replica_groups=mesh['gx'=32,'gy'=8] {'gx','gy'}, use_global_device_ids=true, to_apply=%region_5.6 | all-reduce | flops 1 | bytes 8 | tf_op jit(solution)/shard_map/psum | solution.py:63
  237.6 2.9 collective-permute-start.5
  240.5 1.0 collective-permute-done.5
  241.5 5.1 collective-permute-done.4
  246.6 2.1 collective-permute-start.7
  248.8 26.5 %all-gather.1 = f32[1,1,4096]{2,1,0:T(1,128)S(1)} all-gather(f32[1,1,128]{2,1,0:T(1,128)S(1)} %slice.528), channel_id=3, replica_groups=mesh['gx'=32,'gy'=8] {'gx'}, dimensions={2}, use_global_device_ids=true | all-gather | bytes 16896 | tf_op jit(solution)/shard_map/all_gather | solution.py:28
  275.2 1.1 gather_fusion.2
  276.6 0.3 scatter.30
  276.9 1.6 scatter.31
  278.5 0.7 multiply_reduce_fusion.1
  279.3 81.5 %psum.45 = f32[]{:T(128)} all-reduce(f32[]{:T(128)} %get-tuple-element.115), channel_id=1, replica_groups=mesh['gx'=32,'gy'=8] {'gx','gy'}, use_global_device_ids=true, to_apply=%region_7.9 | all-reduce | flops 1 | bytes 8 | tf_op jit(solution)/shard_map/psum | solution.py:113
  362.1 0.6 multiply_reduce_fusion
  362.7 2.7 copy.112
  365.3 73.6 %psum.46 = f32[]{:T(128)} all-reduce(f32[]{:T(128)} %multiply_reduce_fusion), channel_id=1, replica_groups=mesh['gx'=32,'gy'=8] {'gx','gy'}, use_global_device_ids=true, to_apply=%region_9.11 | all-reduce | flops 1 | bytes 8 | tf_op jit(solution)/shard_map/psum | solution.py:63
  440.4 3.5 collective-permute-start.9
  443.9 2.7 copy.111
  446.6 2.7 copy.110
  449.2 0.7 collective-permute-done.8
  450.0 2.1 collective-permute-start.11
  452.1 27.4 %all-gather.2 = f32[1,1,4096]{2,1,0:T(1,128)S(1)} all-gather(f32[1,1,128]{2,1,0:T(1,128)S(1)} %slice.538), channel_id=4, replica_groups=mesh['gx'=32,'gy'=8] {'gx'}, dimensions={2}, use_global_device_ids=true | all-gather | bytes 16896 | tf_op jit(solution)/shard_map/all_gather | solution.py:28
  479.6 1.1 gather_fusion.3
  480.9 0.3 scatter.34
  481.3 1.6 scatter.35
  482.9 0.7 fusion.31
  483.6 2.8 copy.109
  486.4 81.5 %psum.47 = f32[]{:T(128)} all-reduce(f32[]{:T(128)} %fusion.31), channel_id=1, replica_groups=mesh['gx'=32,'gy'=8] {'gx','gy'}, use_global_device_ids=true, to_apply=%region_11.13 | all-reduce | flops 1 | bytes 8 | tf_op jit(solution)/shard_map/psum | solution.py:113
  569.3 5.2 select_multiply_fusion
  574.5 2.0 copy-done.5
  576.5 1.6 pad_maximum_fusion.9
  578.2 2.2 pad_maximum_fusion.13
  580.3 2.0 collective-permute-start.13
  582.3 0.2 collective-permute-start.12
  582.5 1.0 collective-permute-done.13
  583.5 4.9 collective-permute-done.12
  588.6 3.6 collective-permute-start.14
  592.2 3.3 fusion
  595.6 4.1 collective-permute-done.15
  599.7 6.8 pad_maximum_fusion
  606.4 42.2 %all-gather.6.cloned.1.call-done = f32[100,1,4096]{0,2,1:T(8,128)} async-done(((f32[100,1,128]{0,2,1:T(8,128)}), f32[100,1,4096]{0,2,1:T(8,128)}) %all-gather.6.cloned.1.call-update) | async-done | bytes 1638416 | tf_op jit(solution)/shard_map/all_gather | solution.py:28
  648.6 2.2 gather_fusion.1
  651.0 1.5 scatter.36
  652.5 2.8 scatter.39
  655.2 46.5 %fusion.4 = f32[25,64,128]{0,2,1:T(8,128)} fusion(f32[100,66,130]{0,2,1:T(8,128)} %scatter.39, f32[25,66,130]{0,2,1:T(8,128)} %fusion, f32[25,64,128]{0,2,1:T(8,128)} %copy.109, f32[64,128]{1,0:T(8,128)S(1)} %multiply_add_fusion.1, f32[25]{0:T(128)S(1)} %copy-done.15, f32[64,128]{1,0:T(8,128)S(1)} %get-tuple-element.139), kind=kLoop, calls=%fused_computation.11 | loop fusion | flops 9011200 | bytes 18907236 | tf_op jit(solution)/shard_map/add | solution.py:83
  701.8 3.7 copy.114
  (86 shorter events, 2.7 us)
Async XLA Ops:
  7.2 76.6 %copy-start.12 = (s32[64,128]{1,0:T(8,128)S(1)}, s32[64,128]{1,0:T(8,128)}, u32[]{:S(2)}) copy-start(s32[64,128]{1,0:T(8,128)} %param.32) | copy-start | bytes 98308
  7.2 76.6 %copy-start.7 = (f32[64,128]{1,0:T(8,128)S(1)}, f32[64,128]{1,0:T(8,128)}, u32[]{:S(2)}) copy-start(f32[64,128]{1,0:T(8,128)} %param.27) | copy-start | bytes 98308
  7.2 641.4 %all-gather.6.cloned.1.call-start = ((), (), s32[]{:S(2)}) async-start(), calls=%async_computation | async-start | bytes 2162688 | tf_op jit(solution)/shard_map/all_gather | solution.py:28
  8.0 268.5 %copy-start.14 = (s32[128]{0:T(128)S(1)}, s32[128]{0:T(128)}, u32[]{:S(2)}) copy-start(s32[128]{0:T(128)} %param.33) | copy-start | bytes 1540
  8.9 11.7 %collective-permute-start.1 = (f32[2,64,1]{2,1,0:T(8,128)S(1)}, f32[2,64,1]{2,1,0:T(8,128)S(1)}, u32[]{:S(2)}, u32[]{:S(2)}) collective-permute-start(f32[2,64,1]{2,1,0:T(8,128)S(1)} %get-tuple-element.138), channel_id=1, source_target_pairs={{8,0},{16,8},{24,16},{32,24},{40,32},{48,40},{56,48},{64,56},{72,6... | collective-permute-start | bytes 1544 | tf_op jit(solution)/shard_map/ppermute | solution.py:22
  17.8 6.4 collective-permute-start
  25.2 337.5 %copy-start.8 = (f32[25,64,128]{2,1,0:T(8,128)S(1)}, f32[25,64,128]{2,1,0:T(8,128)}, u32[]{:S(2)}) copy-start(f32[25,64,128]{2,1,0:T(8,128)} %param.30) | copy-start | bytes 2457604
  25.3 52.7 %collective-permute-start.3 = (f32[2,1,130]{0,2,1:T(8,128)S(1)}, f32[2,1,130]{0,2,1:T(8,128)S(1)}, u32[]{:S(2)}, u32[]{:S(2)}) collective-permute-start(f32[2,1,130]{0,2,1:T(8,128)S(1)} %copy.115), channel_id=1, source_target_pairs={{1,0},{2,1},{3,2},{4,3},{5,4},{6,5},{7,6},{0,7},{9,8},{10,9},{11,1... | collective-permute-start | bytes 3128 | tf_op jit(solution)/shard_map/ppermute | solution.py:22
  65.3 14.8 %collective-permute-start.2 = (f32[2,1,130]{1,2,0:T(8,128)S(1)}, f32[2,1,130]{1,2,0:T(8,128)S(1)}, u32[]{:S(2)}, u32[]{:S(2)}) collective-permute-start(f32[2,1,130]{1,2,0:T(8,128)S(1)} %copy.94), channel_id=1, source_target_pairs={{0,1},{1,2},{2,3},{3,4},{4,5},{5,6},{6,7},{7,0},{8,9},{9,10},{10,1... | collective-permute-start | bytes 3128 | tf_op jit(solution)/shard_map/ppermute | solution.py:21
  83.1 360.8 %copy-start.9 = (f32[25,64,128]{2,1,0:T(8,128)S(1)}, f32[25,64,128]{2,1,0:T(8,128)}, u32[]{:S(2)}) copy-start(f32[25,64,128]{2,1,0:T(8,128)} %param.29) | copy-start | bytes 2457604
  237.6 3.9 collective-permute-start.5
  240.5 6.1 collective-permute-start.4
  246.6 29.7 %collective-permute-start.7 = (f32[1,1,130]{2,1,0:T(1,128)S(1)}, f32[1,1,130]{2,1,0:T(1,128)S(1)}, u32[]{:S(2)}, u32[]{:S(2)}) collective-permute-start(f32[1,1,130]{2,1,0:T(1,128)S(1)} %get-tuple-element.131), channel_id=1, source_target_pairs={{1,0},{2,1},{3,2},{4,3},{5,4},{6,5},{7,6},{0,7},{9,8},{10,9},{11,1... | collective-permute-start | bytes 1568 | tf_op jit(solution)/shard_map/ppermute | solution.py:22
  248.7 27.6 %collective-permute-start.6 = (f32[1,1,130]{2,1,0:T(1,128)S(1)}, f32[1,1,130]{2,1,0:T(1,128)S(1)}, u32[]{:S(2)}, u32[]{:S(2)}) collective-permute-start(f32[1,1,130]{2,1,0:T(1,128)S(1)} %get-tuple-element.130), channel_id=1, source_target_pairs={{0,1},{1,2},{2,3},{3,4},{4,5},{5,6},{6,7},{7,0},{8,9},{9,10},{10,1... | collective-permute-start | bytes 1568 | tf_op jit(solution)/shard_map/ppermute | solution.py:21
  362.7 83.9 %copy-start.10 = (f32[25,64,128]{2,1,0:T(8,128)S(1)}, f32[25,64,128]{2,1,0:T(8,128)}, u32[]{:S(2)}) copy-start(f32[25,64,128]{2,1,0:T(8,128)} %param.28) | copy-start | bytes 2457604
  440.4 8.9 %collective-permute-start.9 = (f32[1,64,1]{2,1,0:T(8,128)S(1)}, f32[1,64,1]{2,1,0:T(8,128)S(1)}, u32[]{:S(2)}, u32[]{:S(2)}) collective-permute-start(f32[1,64,1]{2,1,0:T(8,128)S(1)} %get-tuple-element.142), channel_id=1, source_target_pairs={{8,0},{16,8},{24,16},{32,24},{40,32},{48,40},{56,48},{64,56},{72,6... | collective-permute-start | bytes 776 | tf_op jit(solution)/shard_map/ppermute | solution.py:22
  443.9 6.1 collective-permute-start.8
  446.6 37.1 %copy-start.11 = (f32[25,64,128]{2,1,0:T(8,128)S(1)}, f32[25,64,128]{2,1,0:T(8,128)}, u32[]{:S(2)}) copy-start(f32[25,64,128]{2,1,0:T(8,128)} %param.26) | copy-start | bytes 2457604
  449.2 120.1 %copy-start.15 = (f32[25]{0:T(128)S(1)}, f32[25]{0:T(128)}, u32[]{:S(2)}) copy-start(f32[25]{0:T(128)} %param.31) | copy-start | bytes 304
  450.0 30.7 %collective-permute-start.11 = (f32[1,1,130]{2,1,0:T(1,128)S(1)}, f32[1,1,130]{2,1,0:T(1,128)S(1)}, u32[]{:S(2)}, u32[]{:S(2)}) collective-permute-start(f32[1,1,130]{2,1,0:T(1,128)S(1)} %get-tuple-element.129), channel_id=1, source_target_pairs={{1,0},{2,1},{3,2},{4,3},{5,4},{6,5},{7,6},{0,7},{9,8},{10,9},{11,1... | collective-permute-start | bytes 1568 | tf_op jit(solution)/shard_map/ppermute | solution.py:22
  452.1 28.6 %collective-permute-start.10 = (f32[1,1,130]{2,1,0:T(1,128)S(1)}, f32[1,1,130]{2,1,0:T(1,128)S(1)}, u32[]{:S(2)}, u32[]{:S(2)}) collective-permute-start(f32[1,1,130]{2,1,0:T(1,128)S(1)} %get-tuple-element.128), channel_id=1, source_target_pairs={{0,1},{1,2},{2,3},{3,4},{4,5},{5,6},{6,7},{7,0},{8,9},{9,10},{10,1... | collective-permute-start | bytes 1568 | tf_op jit(solution)/shard_map/ppermute | solution.py:21
  569.3 86.0 %copy-start.13 = (f32[64,128]{1,0:T(8,128)}, f32[64,128]{1,0:T(8,128)S(1)}, u32[]{:S(2)}) copy-start(f32[64,128]{1,0:T(8,128)S(1)} %multiply_add_fusion.1) | copy-start | bytes 98308
  569.3 7.2 %copy-start = (f32[25,64,128]{0,2,1:T(8,128)S(1)}, f32[25,64,128]{0,2,1:T(8,128)}, u32[]{:S(2)}) copy-start(f32[25,64,128]{0,2,1:T(8,128)} %copy.112) | copy-start | bytes 2457604
  569.3 7.2 %copy-start.2 = (f32[25,64,128]{0,2,1:T(8,128)S(1)}, f32[25,64,128]{0,2,1:T(8,128)}, u32[]{:S(2)}) copy-start(f32[25,64,128]{0,2,1:T(8,128)} %copy.111) | copy-start | bytes 2457604
  574.5 2.0 copy-start.5
  578.1 10.3 %copy-start.1 = (f32[25,64,128]{0,2,1:T(8,128)S(1)}, f32[25,64,128]{0,2,1:T(8,128)}, u32[]{:S(2)}) copy-start(f32[25,64,128]{0,2,1:T(8,128)} %copy.112) | copy-start | bytes 2457604
  578.2 10.2 %copy-start.3 = (f32[25,64,128]{0,2,1:T(8,128)S(1)}, f32[25,64,128]{0,2,1:T(8,128)}, u32[]{:S(2)}) copy-start(f32[25,64,128]{0,2,1:T(8,128)} %copy.111) | copy-start | bytes 2457604
  578.2 10.2 %copy-start.4 = (f32[25,64,128]{0,2,1:T(8,128)S(1)}, f32[25,64,128]{0,2,1:T(8,128)}, u32[]{:S(2)}) copy-start(f32[25,64,128]{0,2,1:T(8,128)} %copy.110) | copy-start | bytes 2457604
  578.2 10.2 %copy-start.6 = (f32[25,64,128]{0,2,1:T(8,128)S(1)}, f32[25,64,128]{0,2,1:T(8,128)}, u32[]{:S(2)}) copy-start(f32[25,64,128]{0,2,1:T(8,128)} %copy-done.5) | copy-start | bytes 2457604
  580.3 3.2 collective-permute-start.13
  582.3 6.1 collective-permute-start.12
  588.6 6.9 collective-permute-start.14
  595.5 4.1 collective-permute-start.15
  595.6 55.3 %copy-start.16 = (f32[100]{0:T(128)S(1)}, f32[100]{0:T(128)}, u32[]{:S(2)}) copy-start(f32[100]{0:T(128)} %constant.256.clone.1) | copy-start | bytes 1204
Sparse Core Ops, SparseCore 0:
  578.3 70.3 all-gather.5
where the time goes:
time: 717 us; the launch traced here: 712 us
  blocking collectives  477 us (67%)
  other arithmetic  74.7 us (10%)
  waiting for transfers between devices  62.8 us (9%)
  starting transfers between devices  40.2 us (6%)
  local copies, waits for them, and re-layouts  36.4 us (5%)
  between operations  21.2 us (3%)
    psum x3, blocking collectives, squares(): return lax.psum(jnp.sum(residual * residual), ('gx', 'gy'))  223 us
    psum x2, blocking collectives, local(): alpha = norm_now / lax.psum(jnp.sum(direction * image), ('gx', 'gy'))  163 us
    all_gather x3, blocking collectives, mirror_row(): whole_row = lax.all_gather(top_row, 'gx', axis=1, tiled=True)  90.8 us
    add x1, other arithmetic, adjoint_levels(): return total + east + west + north + south  46.5 us
    all_gather x1, waiting for transfers between devices, mirror_row(): whole_row = lax.all_gather(top_row, 'gx', axis=1, tiled=True)  42.2 us
    ppermute x8, starting transfers between devices, with_halo(): after = lax.ppermute(initial, axis, down)  23.6 us
    unnamed x46, local copies, waits for them, and re-layouts  17.2 us
    ppermute x8, starting transfers between devices, with_halo(): before = lax.ppermute(last, axis, up)  16.6 us
  transfers between devices with their start and end apart: 17, of which 9 were waited for; matrix products, arithmetic and copies ran while one was open for 4% of the time, Pallas kernels for 0%

commit v1 on v0

v1 whole, which is shorter than its diff:
```python
import functools

import jax
import jax.numpy as jnp
from jax import lax
from jax.experimental import pallas as pl
from jax.experimental.pallas import tpu as pltpu
from jax.sharding import PartitionSpec as P

MESH = pl.DeviceIdType.MESH
damping = 0.1
time_step = 0.3
ROWS = 64
LANES = 128
PAD = 16
FOLD = 56


def roll_lanes(x, shift):
    return pltpu.roll(x, shift, 1)


def kernel(
    nz, ny, nc, nx, levels,
    cot_h, b_h, u_h, v_h, k_h, th_s, dep_h, fp_s, out_h, hadj_h,
    cot, u, v, kap, dint, plane, wide, pack2, got2, dmin, vec1, vec2,
    edge_ew, got_ew, edge_n, edge_s, got_n, got_s,
    mir2, all2, foldz, fold_stage, fold_y, fold_rows,
    qn, qs, coef_e, coef_w, coef_n, coef_s, base, outv, hv,
    mom, red1, mom2, red2, tot,
    load_sem, store_sem, send_sem, halo_sem, edge_sem, red_sem, fold_sem,
):
    gx, gy = lax.axis_index("gx"), lax.axis_index("gy")
    ngx, ngy = ny * nz, nx * nc
    y, z, x, c = gx // nz, gx % nz, gy // nc, gy % nc
    top = gy == ngy - 1
    lane = lax.broadcasted_iota(jnp.int32, (ROWS, LANES), 1)
    lane80 = lax.broadcasted_iota(jnp.int32, (80, LANES), 1)
    f32 = jnp.float32

    def at(dx, dy):
        return (gx + dx + ngx) % ngx, (gy + dy + ngy) % ngy

    compass = [(1, 0), (-1, 0), (0, 1), (0, -1), (1, 1), (-1, 1), (1, -1), (-1, -1)]

    loads = [
        pltpu.make_async_copy(b_h, plane.at[0, pl.ds(PAD, ROWS)], load_sem.at[0]),
        pltpu.make_async_copy(dep_h, dint, load_sem.at[1]),
        pltpu.make_async_copy(cot_h, cot.at[:, pl.ds(8, ROWS)], load_sem.at[2]),
        pltpu.make_async_copy(u_h, u, load_sem.at[3]),
        pltpu.make_async_copy(k_h, kap, load_sem.at[4]),
        pltpu.make_async_copy(v_h, v, load_sem.at[5]),
    ]
    for load in loads:
        load.start()

    barrier = pltpu.get_barrier_semaphore()

    def greet(device):
        pl.semaphore_signal(barrier, inc=1, device_id=device, device_id_type=MESH)

    n1, n2 = nz * nc, nx * ny
    me1, me2 = z * nc + c, x * ny + y

    def peer1(j):
        p = (me1 + j) % n1
        return y * nz + p // nc, x * nc + p % nc

    def peer2(j):
        p = (me2 + j) % n2
        return (p % ny) * nz + z, (p // ny) * nc + c

    for d in compass:
        greet(at(*d))

    @pl.loop(1, n1)
    def _(j):
        greet(peer1(j))

    @pl.loop(1, n2)
    def _(j):
        greet(peer2(j))

    @pl.when(top)
    def _():
        @pl.loop(1, ngx)
        def _(j):
            greet(at(j, 0))

    zero8 = jnp.zeros((8, LANES), f32)
    for f in range(2):
        for part in (plane, wide, vec1, vec2):
            part[f, 0:8] = zero8
            part[f, 88:96] = zero8
    loads[0].wait()
    loads[1].wait()
    depth_f = dint[...].astype(f32)
    plane[1, PAD:PAD + ROWS] = depth_f
    pack2[...] = jnp.where(
        (lane < 32) | (lane >= 96), plane[0, PAD:PAD + ROWS], roll_lanes(depth_f, 64)
    )

    pl.semaphore_wait(barrier, 8 + n1 - 1 + n2 - 1 + jnp.where(top, ngx - 1, 0))

    def send(src, dst, sem_out, sem_in, device):
        copy = pltpu.make_async_remote_copy(
            src_ref=src, dst_ref=dst, send_sem=sem_out, recv_sem=sem_in,
            device_id=device, device_id_type=MESH,
        )
        return copy

    first, last = pl.ds(PAD, 8), pl.ds(PAD + ROWS - 8, 8)
    south, north = pl.ds(PAD - 8, 8), pl.ds(PAD + ROWS, 8)
    halos = []
    for i, (dx, dy) in enumerate(compass):
        if dx == 0:
            src = plane.at[:, last if dy == 1 else first]
            dst = plane.at[:, south if dy == 1 else north]
        else:
            side = 0 if dx == 1 else 1
            if dy == 0:
                src, dst = pack2, got2.at[side, pl.ds(8, ROWS)]
            elif dy == 1:
                src, dst = pack2.at[pl.ds(ROWS - 8, 8)], got2.at[side, pl.ds(0, 8)]
            else:
                src, dst = pack2.at[pl.ds(0, 8)], got2.at[side, pl.ds(ROWS + 8, 8)]
        halos.append(send(src, dst, send_sem.at[i], halo_sem.at[i], at(dx, dy)))

    @pl.when(top)
    def _():
        for j in range(3):
            row = PAD + ROWS - 1 - j
            mir2[j:j + 1] = plane[0, row:row + 1]
            mir2[3 + j:4 + j] = plane[1, row:row + 1]
        mir2[6:8] = jnp.zeros((2, LANES), f32)
        all2[pl.ds(gx, 1)] = mir2[...][None]

        @pl.loop(1, ngx)
        def _(j):
            send(mir2, all2.at[gx], fold_sem.at[0], fold_sem.at[1], at(j, 0)).start()

    for halo in halos:
        halo.start()

    for load in loads[2:]:
        load.wait()
    half = jnp.where(lane < 64, 0.5, -0.5).astype(f32)
    edge_n[2 * levels:FOLD] = jnp.zeros((FOLD - 2 * levels, LANES), f32)
    edge_s[2 * levels:FOLD] = jnp.zeros((FOLD - 2 * levels, LANES), f32)

    def pack_level(k, acc):
        face = 0.25 * u[k] + half * kap[k]
        place = lane >> 1
        acc = jnp.where(place == k, roll_lanes(cot[k, 8:8 + ROWS], 2 * k + 1), acc)
        acc = jnp.where(place == k + 32, roll_lanes(face, 2 * k + 65), acc)
        edge_n[pl.ds(k, 1)] = cot[k, 7 + ROWS:8 + ROWS]
        edge_s[pl.ds(k, 1)] = cot[k, 8:9]
        edge_n[pl.ds(levels + k, 1)] = 0.25 * v[k, ROWS - 1:ROWS] - 0.5 * kap[k, ROWS - 1:ROWS]
        edge_s[pl.ds(levels + k, 1)] = 0.25 * v[k, 0:1] + 0.5 * kap[k, 0:1]
        return acc

    edge_ew[...] = lax.fori_loop(0, levels, pack_level, jnp.zeros((ROWS, LANES), f32))
    edges = [
        send(edge_ew, got_ew.at[0], send_sem.at[8], edge_sem.at[0], at(1, 0)),
        send(edge_ew, got_ew.at[1], send_sem.at[9], edge_sem.at[1], at(-1, 0)),
        send(edge_n, got_s, send_sem.at[10], edge_sem.at[2], at(0, 1)),
        send(edge_s, got_n, send_sem.at[11], edge_sem.at[3], at(0, -1)),
    ]
    for edge in edges:
        edge.start()

    @pl.when(top)
    def _():
        foldz[pl.ds(z, 1)] = edge_n[...][None]

        @pl.loop(1, nz)
        def _(j):
            p = y * nz + (z + j) % nz
            send(edge_n, foldz.at[z], fold_sem.at[2], fold_sem.at[3], (p, gy)).start()

    for halo in halos:
        halo.wait_recv()
    hw, he = got2[0], got2[1]
    wide[0, 8:88] = jnp.where(lane80 < 64, he, hw)
    wide[1, 8:88] = roll_lanes(jnp.where(lane80 < 64, hw, he), 64)

    seam = fp_s[0] + gx * LANES + 1

    @pl.when(gy == 0)
    def _():
        plane[1, 8:16] = zero8
        wide[1, 8:16] = zero8

    @pl.when(top)
    def _():
        pltpu.make_async_copy(all2.at[pl.ds(0, ngx - 1)], all2.at[pl.ds(0, ngx - 1)], fold_sem.at[1]).wait()
        start = (seam - 1 - gx * LANES - (LANES + 2) + 2 * ngx * LANES) % (ngx * LANES)
        blk, off = start // LANES, start % LANES
        window = jnp.concatenate([all2[(blk + i) % ngx] for i in range(3)], axis=1)
        col = lax.broadcasted_iota(jnp.int32, (3 * LANES, 2 * LANES), 1)
        src = lax.broadcasted_iota(jnp.int32, (3 * LANES, 2 * LANES), 0)
        col = jnp.where(col < 192, col, col - 256)
        pick = (src == off + (LANES + 2) - col).astype(f32)
        got = lax.dot(window, pick, precision=lax.Precision.HIGHEST, preferred_element_type=f32)
        edge_row = PAD + ROWS
        plane[0, edge_row:edge_row + 3] = got[0:3, :LANES]
        wide[0, edge_row:edge_row + 3] = got[0:3, LANES:]
        plane[1, edge_row:edge_row + 3] = got[3:6, :LANES]
        wide[1, edge_row:edge_row + 3] = got[3:6, LANES:]

    first_lane, last_lane = lane80 == 0, lane80 == LANES - 1

    def neighbours(mid, beside, rows):
        return [
            jnp.where(last_lane[:rows], roll_lanes(beside, LANES - 1), roll_lanes(mid, LANES - 1)),
            jnp.where(first_lane[:rows], roll_lanes(beside, 1), roll_lanes(mid, 1)),
        ]

    def both(mid, beside):
        return neighbours(mid, beside, 80), neighbours(beside, mid, 80)

    body, up, down = pl.ds(8, 80), pl.ds(9, 80), pl.ds(7, 80)
    dm, db = plane[1, body], wide[1, body]
    (d_e, d_w), (db_e, db_w) = both(dm, db)
    for i, (a, o) in enumerate(
        [(d_e, db_e), (d_w, db_w), (plane[1, up], wide[1, up]), (plane[1, down], wide[1, down])]
    ):
        dmin[i, 0] = jnp.minimum(dm, a)
        dmin[i, 1] = jnp.minimum(db, o)

    def apply(mid_ref, beside_ref, out_ref):
        mid, beside = mid_ref[body], beside_ref[body]
        (m_e, m_w), (s_e, s_w) = both(mid, beside)
        for i, (centre, nbrs) in enumerate(
            [
                (mid, (m_e, m_w, mid_ref[up], mid_ref[down])),
                (beside, (s_e, s_w, beside_ref[up], beside_ref[down])),
            ]
        ):
            total = jnp.zeros_like(centre)
            for j in range(4):
                total = total + dmin[j, i] * (centre - nbrs[j])
            out_ref[i, body] = damping * centre + (1.0 / levels) * total

    apply(plane.at[0], wide.at[0], vec1)
    apply(vec1.at[0], vec1.at[1], vec2)
    inner = pl.ds(PAD, ROWS)
    mid2 = vec2[0, inner]
    m_e, m_w = neighbours(mid2, vec2[1, inner], ROWS)
    nbrs = (m_e, m_w, vec2[0, PAD + 1:PAD + 1 + ROWS], vec2[0, PAD - 1:PAD - 1 + ROWS])
    mid3 = jnp.zeros_like(mid2)
    for j in range(4):
        mid3 = mid3 + dmin[j, 0, 8:8 + ROWS] * (mid2 - nbrs[j])
    mid3 = damping * mid2 + (1.0 / levels) * mid3
    mid0, mid1 = plane[0, inner], vec1[0, inner]

    def tile_sum(a):
        s = a[0:8]
        for i in range(1, ROWS // 8):
            s = s + a[8 * i:8 * i + 8]
        return jnp.sum(s, axis=0, keepdims=True)

    for j, (a, o) in enumerate(
        [(mid0, mid0), (mid0, mid1), (mid1, mid1), (mid1, mid2), (mid2, mid2), (mid2, mid3)]
    ):
        mom[j:j + 1] = tile_sum(a * o)
    mom[6:8] = jnp.zeros((2, LANES), f32)
    mom[...] = jnp.broadcast_to(jnp.sum(mom[...], axis=1, keepdims=True), (8, LANES))

    red1[pl.ds(me1, 1)] = mom[...][None]

    @pl.loop(1, n1)
    def _(j):
        send(mom, red1.at[me1], red_sem.at[0], red_sem.at[1], peer1(j)).start()

    for edge in edges:
        edge.wait_recv()

    @pl.when(top)
    def _():
        pltpu.make_async_copy(foldz.at[pl.ds(0, nz - 1)], foldz.at[pl.ds(0, nz - 1)], fold_sem.at[3]).wait()
        start = (seam - 1 - gx * LANES - (LANES - 1) + 2 * ngx * LANES) % (ngx * LANES)
        blk, off = start // LANES, start % LANES
        fold_stage[0] = foldz[blk % nz]
        fold_stage[1] = foldz[(blk + 1) % nz]
        fold_y[pl.ds(y, 1)] = fold_stage[...][None]

        @pl.loop(1, ny)
        def _(j):
            p = ((y + j) % ny) * nz + z
            send(fold_stage, fold_y.at[y], fold_sem.at[4], fold_sem.at[5], (p, gy)).start()

    def wait_red(buf, n, sem):
        pltpu.make_async_copy(buf.at[pl.ds(0, n - 1)], buf.at[pl.ds(0, n - 1)], sem).wait()

    def total_of(buf, n):
        parts = [buf[i] for i in range(n)]
        while len(parts) > 1:
            parts = [parts[i] + parts[i + 1] if i + 1 < len(parts) else parts[i] for i in range(0, len(parts), 2)]
        return parts[0]

    wait_red(red1, n1, red_sem.at[1])
    mom2[...] = total_of(red1, n1)
    red2[pl.ds(me2, 1)] = mom2[...][None]

    @pl.loop(1, n2)
    def _(j):
        send(mom2, red2.at[me2], red_sem.at[2], red_sem.at[3], peer2(j)).start()

    @pl.when(top)
    def _():
        pltpu.make_async_copy(fold_y.at[pl.ds(0, ny - 1)], fold_y.at[pl.ds(0, ny - 1)], fold_sem.at[5]).wait()
        start = (seam - 1 - gx * LANES - (LANES - 1) + 2 * ngx * LANES) % (ngx * LANES)
        blk, off = start // LANES, start % LANES
        after = (blk + 1) % ngx
        window = jnp.concatenate([fold_y[blk // nz, 0], fold_y[after // nz, 1]], axis=1)
        col = lax.broadcasted_iota(jnp.int32, (2 * LANES, LANES), 1)
        src = lax.broadcasted_iota(jnp.int32, (2 * LANES, LANES), 0)
        pick = (src == off + (LANES - 1) - col).astype(f32)
        got = lax.dot(window, pick, precision=lax.Precision.HIGHEST, preferred_element_type=f32)
        row = lax.broadcasted_iota(jnp.int32, (FOLD, LANES), 0)
        got_n[...] = jnp.where(row < levels, got, -got)

    fold_rows[...] = jnp.where((lane & 1) == 1, got_ew[1], got_ew[0])
    lane16 = lax.broadcasted_iota(jnp.int32, (16, LANES), 1)

    def level(k, carry):
        kf = k.astype(f32)
        cot[k, 7:8] = got_s[pl.ds(k, 1)]
        cot[k, 8 + ROWS:9 + ROWS] = got_n[pl.ds(k, 1)]
        qs[7:8] = got_s[pl.ds(levels + k, 1)]
        qn[8 + ROWS:9 + ROWS] = got_n[pl.ds(levels + k, 1)]
        for r in range(0, ROWS, 16):
            rows = slice(r, r + 16)
            vq, kq = 0.25 * v[k, rows], 0.5 * kap[k, rows]
            qn[8 + r:24 + r] = vq + kq
            qs[8 + r:24 + r] = vq - kq
        for r in range(0, ROWS, 16):
            rows, mid = slice(r, r + 16), slice(8 + r, 24 + r)
            ct = cot[k, mid]
            uq, kq = 0.25 * u[k, rows], 0.5 * kap[k, rows]
            qe, qw = uq + kq, uq - kq
            edge = fold_rows[rows]
            ec = roll_lanes(edge, (LANES - 1) - 2 * k)
            eq = roll_lanes(edge, 63 - 2 * k)
            c_e = roll_lanes(jnp.where(lane16 == 0, ec, ct), LANES - 1)
            c_w = roll_lanes(jnp.where(lane16 == LANES - 1, ec, ct), 1)
            q_e = roll_lanes(jnp.where(lane16 == 0, eq, qe), LANES - 1)
            q_w = roll_lanes(jnp.where(lane16 == LANES - 1, eq, qw), 1)
            c_n, c_s = cot[k, 9 + r:25 + r], cot[k, 7 + r:23 + r]
            ke = jnp.where(dmin[0, 0, mid] > kf, time_step * (qe + q_e), 0.0)
            kw = jnp.where(dmin[1, 0, mid] > kf, time_step * (qw + q_w), 0.0)
            kn = jnp.where(dmin[2, 0, mid] > kf, time_step * (qn[8 + r:24 + r] + qn[9 + r:25 + r]), 0.0)
            ks = jnp.where(dmin[3, 0, mid] > kf, time_step * (qs[8 + r:24 + r] + qs[7 + r:23 + r]), 0.0)
            coef_e[k, rows], coef_w[k, rows], coef_n[k, rows], coef_s[k, rows] = ke, kw, kn, ks
            base[k, rows] = ct + (ke * (c_e - ct) + kw * (ct - c_w)) + (kn * (c_n - ct) + ks * (ct - c_s))
        return carry

    lax.fori_loop(0, levels, level, 0)

    wait_red(red2, n2, red_sem.at[3])
    tot[...] = total_of(red2, n2)
    m = [jnp.broadcast_to(tot[j:j + 1], (8, LANES)) for j in range(6)]
    lo, hi = 0.0999, 8.2
    rho = m[1] / m[0]
    s1 = [m[j + 1] - rho * m[j] for j in range(5)]
    n = [s1[j + 1] - rho * s1[j] for j in range(4)]
    n[0] = jnp.maximum(n[0], 0.0)

    def bounded(t, least, most):
        return jnp.where(t >= least, jnp.minimum(t, most), least)

    e1 = n[0] / m[0]
    rho1 = bounded(n[1] / n[0], lo, hi)
    p1 = bounded(rho1 - e1 / rho, lo, hi)
    k0 = n[2] - rho1 * n[1] - e1 * n[0]
    k1 = n[3] - 2.0 * rho1 * n[2] + rho1 * rho1 * n[1] - 2.0 * e1 * rho * n[0] + e1 * e1 * m[1]
    e2 = bounded(k0 / n[0], 0.0, 70.0)
    rho2 = bounded(k1 / k0, lo, hi)
    p2 = bounded(rho2 - e2 / p1, lo, hi)
    z0 = 1.0 / rho
    z1 = -z0 / p1
    y2 = -z1 / p2
    y1 = z1 - e2 / p1 * y2
    y0 = z0 - e1 / rho * y1
    a0 = y0 - rho * y1 + (rho1 * rho - e1) * y2
    a1 = y1 - (rho + rho1) * y2

    def spread(a, rows):
        return jnp.broadcast_to(a[0:1], (rows, LANES))

    rows80 = [spread(a, 80) for a in (a0, a1, y2)]
    h_mid = rows80[0] * plane[0, body] + rows80[1] * vec1[0, body] + rows80[2] * vec2[0, body]
    h_side = rows80[0] * wide[0, body] + rows80[1] * vec1[1, body] + rows80[2] * vec2[1, body]
    hv[0, body] = h_mid
    inner_mid, inner_side = h_mid[8:8 + ROWS], h_side[8:8 + ROWS]
    h_e, h_w = neighbours(inner_mid, inner_side, ROWS)
    hv[1, inner] = h_e - inner_mid
    hv[2, inner] = inner_mid - h_w
    hv[3, inner] = hv[0, PAD + 1:PAD + 1 + ROWS] - inner_mid
    hv[4, inner] = inner_mid - hv[0, PAD - 1:PAD - 1 + ROWS]
    height = pltpu.make_async_copy(hv.at[0, inner], hadj_h, store_sem.at[0])
    height.start()
    stores = []
    for r in range(0, ROWS, 8):
        rows, mid = slice(r, r + 8), slice(PAD + r, PAD + r + 8)
        hc, de, dw, dn, ds_ = [hv[i, mid] for i in range(5)]
        wet = plane[1, mid]

        def finish(k, carry):
            grown = (
                jnp.where(wet > k.astype(f32), hc, 0.0)
                + (coef_e[k, rows] * de + coef_w[k, rows] * dw)
                + (coef_n[k, rows] * dn + coef_s[k, rows] * ds_)
            )
            outv[k, rows] = base[k, rows] + th_s[k] * grown
            return carry

        lax.fori_loop(0, levels, finish, 0, unroll=5)
        store = pltpu.make_async_copy(
            outv.at[:, pl.ds(r, 8)], out_h.at[:, pl.ds(r, 8)], store_sem.at[1 + r // 8]
        )
        store.start()
        stores.append(store)

    for halo in halos:
        halo.wait_send()
    for edge in edges:
        edge.wait_send()
    wait_red(red1, n1, red_sem.at[0])
    wait_red(red2, n2, red_sem.at[2])

    @pl.when(top)
    def _():
        pltpu.make_async_copy(all2.at[pl.ds(0, ngx - 1)], all2.at[pl.ds(0, ngx - 1)], fold_sem.at[0]).wait()
        pltpu.make_async_copy(foldz.at[pl.ds(0, nz - 1)], foldz.at[pl.ds(0, nz - 1)], fold_sem.at[2]).wait()
        pltpu.make_async_copy(fold_y.at[pl.ds(0, ny - 1)], fold_y.at[pl.ds(0, ny - 1)], fold_sem.at[4]).wait()

    height.wait()
    for store in stores:
        store.wait()


def solution(mesh):
    ngx, ngy = mesh.shape["gx"], mesh.shape["gy"]
    nc = 2
    nx = ngy // nc
    ny = 4 if ngx == 32 else 2
    nz = ngx // ny

    def local(cot, b, u, v, kap, th, dep, fp):
        levels = cot.shape[0]
        f32 = jnp.float32

        def vmem(*shape, dtype=f32):
            return pltpu.VMEM(shape, dtype)

        n1, n2 = nz * nc, nx * ny
        cube = (levels, ROWS, LANES)
        scratch = [
            vmem(levels, 80, LANES), vmem(*cube), vmem(*cube), vmem(*cube),
            vmem(ROWS, LANES, dtype=jnp.int32),
            vmem(2, 96, LANES), vmem(2, 96, LANES),
            vmem(ROWS, LANES), vmem(2, 80, LANES), vmem(4, 2, 80, LANES),
            vmem(2, 96, LANES), vmem(2, 96, LANES),
            vmem(ROWS, LANES), vmem(2, ROWS, LANES),
            vmem(FOLD, LANES), vmem(FOLD, LANES), vmem(FOLD, LANES), vmem(FOLD, LANES),
            vmem(8, LANES), vmem(ngx, 8, LANES),
            vmem(nz, FOLD, LANES), vmem(2, FOLD, LANES), vmem(ny, 2, FOLD, LANES),
            vmem(ROWS, LANES),
            vmem(80, LANES), vmem(80, LANES),
            vmem(*cube), vmem(*cube), vmem(*cube), vmem(*cube), vmem(*cube), vmem(*cube),
            vmem(5, 96, LANES),
            vmem(8, LANES), vmem(n1, 8, LANES), vmem(8, LANES), vmem(n2, 8, LANES), vmem(8, LANES),
            pltpu.SemaphoreType.DMA((6,)), pltpu.SemaphoreType.DMA((9,)),
            pltpu.SemaphoreType.DMA((12,)), pltpu.SemaphoreType.DMA((8,)),
            pltpu.SemaphoreType.DMA((4,)), pltpu.SemaphoreType.DMA((4,)),
            pltpu.SemaphoreType.DMA((6,)),
        ]
        hbm = pl.BlockSpec(memory_space=pl.ANY)
        smem = pl.BlockSpec(memory_space=pltpu.SMEM)
        return pl.pallas_call(
            functools.partial(kernel, nz, ny, nc, nx, levels),
            out_shape=(jax.ShapeDtypeStruct(cube, f32), jax.ShapeDtypeStruct((ROWS, LANES), f32)),
            in_specs=[hbm, hbm, hbm, hbm, hbm, smem, hbm, smem],
            out_specs=(hbm, hbm),
            scratch_shapes=scratch,
            compiler_params=pltpu.CompilerParams(
                collective_id=0, has_side_effects=True, vmem_limit_bytes=40 * 1024 * 1024
            ),
        )(cot, b, u, v, kap, th, dep, fp)

    in_specs = (
        P(None, "gy", "gx"), P("gy", "gx"), P(None, "gy", "gx"), P(None, "gy", "gx"),
        P(None, "gy", "gx"), P(), P("gy", "gx"), P("gx"),
    )
    out_specs = (P(None, "gy", "gx"), P("gy", "gx"))
    return jax.shard_map(local, mesh=mesh, in_specs=in_specs, out_specs=out_specs, check_vma=False)
```

time: 717 us -> 40.8 us (0.06)
  blocking collectives: 477 us -> 0 us
  other arithmetic: 74.7 us -> 0 us
  waiting for transfers between devices: 62.8 us -> 0 us
  starting transfers between devices: 40.2 us -> 0 us
  Pallas kernels: 0 us -> 30.8 us
  local copies, waits for them, and re-layouts: 36.4 us -> 8.9 us
  between operations: 21.2 us -> 0.66 us
    psum x5 -> x0, blocking collectives: 386 us -> none  [the longest x3 223 us: squares(): return lax.psum(jnp.sum(residual * residual), ('gx', 'gy'))]
    all_gather x3 -> x0, blocking collectives: 90.8 us -> none  [mirror_row(): whole_row = lax.all_gather(top_row, 'gx', axis=1, tiled=True)]
    add x4 -> x0, other arithmetic: 46.6 us -> none  [the longest x1 46.5 us: adjoint_levels(): return total + east + west + north + south]
    all_gather x1 -> x0, waiting for transfers between devices: 42.2 us -> none  [mirror_row(): whole_row = lax.all_gather(top_row, 'gx', axis=1, tiled=True)]
    ppermute x16 -> x0, starting transfers between devices: 40.2 us -> none  [the longest x8 23.6 us: with_halo(): after = lax.ppermute(initial, axis, down)]
    pallas_call x0 -> x1, Pallas kernels: none -> 30.8 us  [local(): pl.pallas_call(functools.partial(kernel, nz, ny, nc, nx, levels), out_sha...]
    ppermute x16 -> x0, waiting for transfers between devices: 20.5 us -> none  [the longest x8 14.4 us: with_halo(): before = lax.ppermute(last, axis, up)]
    scatter x8 -> x0, local copies, waits for them, and re-layouts: 10.9 us -> none  [extend_block(): return padded.at[:, -1, 1:-1].set(north).at[:, 0, 1:-1].set(south)]
  transfers between devices with their start and end apart: 17 -> 0, of which waited for: 9 -> 0; matrix products, arithmetic and copies ran while one was open for 4% -> 0% of each run, Pallas kernels for 0% -> 0%
where the time goes in v1:
time: 40.8 us; the launch traced here: 40.4 us
  Pallas kernels  30.8 us (75%)
  local copies, waits for them, and re-layouts  8.9 us (22%)
  between operations  0.66 us (2%)
    pallas_call x1, Pallas kernels, local(): pl.pallas_call(functools.partial(kernel, nz, ny, nc, nx, levels), out_sha...  30.8 us
    unnamed x18, local copies, waits for them, and re-layouts  8.9 us

profile of v1, /device:TPU:1, one launch (start us, length us, event | category | flops | bytes accessed | tf_op | source)
XLA Modules:
  0.0 40.4 jit_solution(14534415759437092825)
XLA Ops:
  0.6 0.0 copy-start
  0.6 1.1 %copy-done = f32[25,64,128]{2,1,0:T(8,128)S(1)} copy-done((f32[25,64,128]{2,1,0:T(8,128)S(1)}, f32[25,64,128]{2,1,0:T(8,128)}, u32[]{:S(2)}) %copy-start) | copy-done | bytes 819224
  1.8 0.0 copy-start.1
  1.8 1.1 %copy-done.1 = f32[25,64,128]{2,1,0:T(8,128)S(1)} copy-done((f32[25,64,128]{2,1,0:T(8,128)S(1)}, f32[25,64,128]{2,1,0:T(8,128)}, u32[]{:S(2)}) %copy-start.1) | copy-done | bytes 819224
  2.9 0.0 copy-start.2
  2.9 1.1 %copy-done.2 = f32[25,64,128]{2,1,0:T(8,128)S(1)} copy-done((f32[25,64,128]{2,1,0:T(8,128)S(1)}, f32[25,64,128]{2,1,0:T(8,128)}, u32[]{:S(2)}) %copy-start.2) | copy-done | bytes 819224
  4.1 0.0 copy-start.3
  4.1 1.1 %copy-done.3 = f32[25,64,128]{2,1,0:T(8,128)S(1)} copy-done((f32[25,64,128]{2,1,0:T(8,128)S(1)}, f32[25,64,128]{2,1,0:T(8,128)}, u32[]{:S(2)}) %copy-start.3) | copy-done | bytes 819224
  5.2 0.0 copy-start.4
  5.2 0.8 %copy-done.4 = f32[64,128]{1,0:T(8,128)S(1)} copy-done((f32[64,128]{1,0:T(8,128)S(1)}, f32[64,128]{1,0:T(8,128)}, u32[]{:S(2)}) %copy-start.4) | copy-done | bytes 32792
  6.0 0.0 copy-start.5
  6.0 0.8 %copy-done.5 = s32[64,128]{1,0:T(8,128)S(1)} copy-done((s32[64,128]{1,0:T(8,128)S(1)}, s32[64,128]{1,0:T(8,128)}, u32[]{:S(2)}) %copy-start.5) | copy-done | bytes 32792
  6.7 0.0 copy-start.6
  6.7 0.7 %copy-done.6 = f32[25]{0:T(128)S(1)} copy-done((f32[25]{0:T(128)S(1)}, f32[25]{0:T(128)}, u32[]{:S(2)}) %copy-start.6) | copy-done | bytes 124
  7.4 0.0 copy-start.7
  7.4 0.7 %copy-done.7 = s32[128]{0:T(128)S(1)} copy-done((s32[128]{0:T(128)S(1)}, s32[128]{0:T(128)}, u32[]{:S(2)}) %copy-start.7) | copy-done | bytes 536
  8.0 30.8 %shard_map.95 = (f32[25,64,128]{2,1,0:T(8,128)S(1)}, f32[64,128]{1,0:T(8,128)S(1)}) custom-call(f32[25,64,128]{2,1,0:T(8,128)S(1)} %copy-done, f32[64,128]{1,0:T(8,128)S(1)} %copy-done.4, f32[25,64,128]{2,1,0:T(8,128)S(1)} %copy-done.1, f32[25,64,128]{2,1,0:T(8,128)S(1)} %copy-done.2, f32[25,64,128]{2,1,0:T(8,128)S(1)} %copy-done.3, f32[25]{0:T(128)S(1)} %copy-done.6, ...), custom_call_target="tpu_custom_call" | custom-call | tf_op jit(solution)/shard_map/pallas_call | solution.py:482
  38.9 0.9 %copy.12 = f32[25,64,128]{2,1,0:T(8,128)} copy(f32[25,64,128]{2,1,0:T(8,128)S(1)} %get-tuple-element.4) | data formatting | bytes 1638400
  39.8 0.6 %copy.13 = f32[64,128]{1,0:T(8,128)} copy(f32[64,128]{1,0:T(8,128)S(1)} %get-tuple-element.5) | data formatting | bytes 65536
Async XLA Ops:
  0.6 1.1 %copy-start = (f32[25,64,128]{2,1,0:T(8,128)S(1)}, f32[25,64,128]{2,1,0:T(8,128)}, u32[]{:S(2)}) copy-start(f32[25,64,128]{2,1,0:T(8,128)} %cot_h.1) | copy-start | bytes 2457604
  1.8 1.1 %copy-start.1 = (f32[25,64,128]{2,1,0:T(8,128)S(1)}, f32[25,64,128]{2,1,0:T(8,128)}, u32[]{:S(2)}) copy-start(f32[25,64,128]{2,1,0:T(8,128)} %u_h.1) | copy-start | bytes 2457604
  2.9 1.1 %copy-start.2 = (f32[25,64,128]{2,1,0:T(8,128)S(1)}, f32[25,64,128]{2,1,0:T(8,128)}, u32[]{:S(2)}) copy-start(f32[25,64,128]{2,1,0:T(8,128)} %v_h.1) | copy-start | bytes 2457604
  4.1 1.1 %copy-start.3 = (f32[25,64,128]{2,1,0:T(8,128)S(1)}, f32[25,64,128]{2,1,0:T(8,128)}, u32[]{:S(2)}) copy-start(f32[25,64,128]{2,1,0:T(8,128)} %k_h.1) | copy-start | bytes 2457604
  5.2 0.8 %copy-start.4 = (f32[64,128]{1,0:T(8,128)S(1)}, f32[64,128]{1,0:T(8,128)}, u32[]{:S(2)}) copy-start(f32[64,128]{1,0:T(8,128)} %b_h.1) | copy-start | bytes 98308
  6.0 0.8 %copy-start.5 = (s32[64,128]{1,0:T(8,128)S(1)}, s32[64,128]{1,0:T(8,128)}, u32[]{:S(2)}) copy-start(s32[64,128]{1,0:T(8,128)} %dep_h.1) | copy-start | bytes 98308
  6.7 0.7 %copy-start.6 = (f32[25]{0:T(128)S(1)}, f32[25]{0:T(128)}, u32[]{:S(2)}) copy-start(f32[25]{0:T(128)} %th_s.1) | copy-start | bytes 304
  7.4 0.7 %copy-start.7 = (s32[128]{0:T(128)S(1)}, s32[128]{0:T(128)}, u32[]{:S(2)}) copy-start(s32[128]{0:T(128)} %fp_s.1) | copy-start | bytes 1540

commit v2 on v1

v2 whole, which is shorter than its diff:
```python
import functools

import jax
import jax.numpy as jnp
from jax import lax
from jax.experimental import pallas as pl
from jax.experimental.pallas import tpu as pltpu
from jax.sharding import PartitionSpec as P

MESH = pl.DeviceIdType.MESH
damping = 0.1
time_step = 0.3
ROWS = 64
LANES = 128
PAD = 16
FOLD = 56


def roll_lanes(x, shift):
    return pltpu.roll(x, shift, 1)


def two_sum(a, b):
    total = a + b
    t = total - a
    return total, (a - (total - t)) + (b - t)


def split(a):
    t = 4097.0 * a
    high = t - (t - a)
    return a, high, a - high


def two_product(a, b):
    (a, ah, al), (b, bh, bl) = a, b
    p = a * b
    return p, ((ah * bh - p) + ah * bl + al * bh) + al * bl


def pair_add(a, b):
    total, rest = two_sum(a[0], b[0])
    return total, rest + (a[1] + b[1])


def renormal(a):
    total = a[0] + a[1]
    return total, a[1] - (total - a[0])


def folded_rows(a):
    rows = a[0].shape[0]
    while rows > 8:
        keep = rows // 2 if rows % 16 == 0 else rows - 8
        rest = pair_add([t[:rows - keep] for t in a], [t[keep:] for t in a])
        a = [jnp.concatenate([t, o[rows - keep:keep]]) if 2 * keep > rows else t for t, o in zip(rest, a)]
        rows = keep
    for shift in (4, 2, 1):
        a = pair_add(a, [pltpu.roll(t, shift, 0) for t in a])
    return a


def kernel(
    nz, ny, nc, nx, levels,
    cot_h, b_h, u_h, v_h, k_h, dep_h, fp_h, faces_h, height_h,
    fp_s, cot, u, v, kap, dint, plane, wide, pack2, got2, dmin, vec1, vec2,
    edge_ew, got_ew, edge_n, edge_s, got_n, got_s,
    top2, all2, mir, foldz, fold_stage, fold_y, sides,
    qn, qs, faces, hv,
    mom, red1, mom2, red2, band, tot,
    load_sem, store_sem, send_sem, halo_sem, edge_sem, red_sem, fold_sem, band_sem,
):
    gx, gy = lax.axis_index("gx"), lax.axis_index("gy")
    ngx, ngy = ny * nz, nx * nc
    y, z, x, c = gx // nz, gx % nz, gy // nc, gy % nc
    top = gy == ngy - 1
    lane = lax.broadcasted_iota(jnp.int32, (ROWS, LANES), 1)
    lane80 = lax.broadcasted_iota(jnp.int32, (80, LANES), 1)
    f32 = jnp.float32

    def at(dx, dy):
        return (gx + dx + ngx) % ngx, (gy + dy + ngy) % ngy

    compass = [(1, 0), (-1, 0), (0, 1), (0, -1), (1, 1), (-1, 1), (1, -1), (-1, -1)]

    loads = [
        pltpu.make_async_copy(b_h, plane.at[0, pl.ds(PAD, ROWS)], load_sem.at[0]),
        pltpu.make_async_copy(dep_h, dint, load_sem.at[1]),
        pltpu.make_async_copy(cot_h, cot.at[:, pl.ds(8, ROWS)], load_sem.at[2]),
        pltpu.make_async_copy(u_h, u, load_sem.at[3]),
        pltpu.make_async_copy(k_h, kap, load_sem.at[4]),
        pltpu.make_async_copy(v_h, v, load_sem.at[5]),
        pltpu.make_async_copy(fp_h, fp_s, load_sem.at[6]),
    ]
    for load in loads:
        load.start()

    barrier = pltpu.get_barrier_semaphore()

    def greet(device):
        pl.semaphore_signal(barrier, inc=1, device_id=device, device_id_type=MESH)

    def far_first(n):
        return sorted(range(n), key=lambda d: (-min(d, n - d), d))

    far_y = [((y + d) % ny) * nz for d in far_first(ny)]
    n1, n2 = nz * nc, nx * ny
    me1, me2 = z * nc + c, y * nx + x
    far_z = [(z + d) % nz for d in far_first(nz)]
    far_yx = sorted(
        [(d, e) for d in range(ny) for e in range(nx)],
        key=lambda t: -min(t[0], ny - t[0]) - min(t[1], nx - t[1]),
    )

    def group1(act):
        for d, pz in zip(far_first(nz), far_z):
            for e in range(nc - 1, -1, -1):
                if (d, e) != (0, 0):
                    act((y * nz + pz, x * nc + (c + e) % nc))

    def group2(act):
        for d, e in far_yx:
            if (d, e) != (0, 0):
                act(((y + d) % ny * nz + z, (x + e) % nx * nc + c))

    def everyone_on_top(act):
        for pz in far_z[:-1]:
            for py in far_y:
                act((py + pz, gy))
        for py in far_y[:-1]:
            act((py + z, gy))

    for d in compass:
        greet(at(*d))
    group1(greet)
    group2(greet)

    @pl.when(top)
    def _():
        everyone_on_top(greet)

    @pl.when(gy != ngy - 1)
    def _():
        greet((gx, ngy - 1))

    zero8 = jnp.zeros((8, LANES), f32)
    for part, n in ((red1, n1), (red2, n2 + 1)):
        if n < part.shape[0]:
            part[n:] = jnp.zeros((part.shape[0] - n, LANES), f32)
    for f in range(2):
        for part in (plane, wide, vec1, vec2):
            part[f, 0:8] = zero8
            part[f, 88:96] = zero8
    loads[0].wait()
    loads[1].wait()
    depth_f = dint[...].astype(f32)
    plane[1, PAD:PAD + ROWS] = depth_f
    pack2[...] = jnp.where(
        (lane < 32) | (lane >= 96), plane[0, PAD:PAD + ROWS], roll_lanes(depth_f, 64)
    )

    pl.semaphore_wait(barrier, 8 + n1 - 1 + n2 - 1 + jnp.where(top, ngx - 1 + ngy - 1, 0))

    def send(src, dst, sem_out, sem_in, device):
        copy = pltpu.make_async_remote_copy(
            src_ref=src, dst_ref=dst, send_sem=sem_out, recv_sem=sem_in,
            device_id=device, device_id_type=MESH,
        )
        return copy

    first, last = pl.ds(PAD, 8), pl.ds(PAD + ROWS - 8, 8)
    south, north = pl.ds(PAD - 8, 8), pl.ds(PAD + ROWS, 8)
    halos = []
    for i, (dx, dy) in enumerate(compass):
        if dx == 0:
            src = plane.at[:, last if dy == 1 else first]
            dst = plane.at[:, south if dy == 1 else north]
        else:
            side = 0 if dx == 1 else 1
            if dy == 0:
                src, dst = pack2, got2.at[side, pl.ds(8, ROWS)]
            elif dy == 1:
                src, dst = pack2.at[pl.ds(ROWS - 8, 8)], got2.at[side, pl.ds(0, 8)]
            else:
                src, dst = pack2.at[pl.ds(0, 8)], got2.at[side, pl.ds(ROWS + 8, 8)]
        halos.append(send(src, dst, send_sem.at[i], halo_sem.at[i], at(dx, dy)))

    @pl.when(top)
    def _():
        top2[0:8] = plane[0, last]
        top2[8:16] = plane[1, last]
        mine = pl.ds(pl.multiple_of(gx * 16, 16), 16)
        all2[mine] = top2[...]
        everyone_on_top(lambda d: send(top2, all2.at[mine], fold_sem.at[0], fold_sem.at[1], d).start())

    for halo in halos:
        halo.start()

    for load in loads[2:6]:
        load.wait()
    half = jnp.where(lane < 64, 0.5, -0.5).astype(f32)
    edge_n[2 * levels:FOLD] = jnp.zeros((FOLD - 2 * levels, LANES), f32)
    edge_s[2 * levels:FOLD] = jnp.zeros((FOLD - 2 * levels, LANES), f32)

    def pack_level(k, acc):
        face = 0.25 * u[k] + half * kap[k]
        place = lane >> 1
        acc = jnp.where(place == k, roll_lanes(cot[k, 8:8 + ROWS], 2 * k + 1), acc)
        acc = jnp.where(place == k + 32, roll_lanes(face, 2 * k + 65), acc)
        edge_n[pl.ds(k, 1)] = cot[k, 7 + ROWS:8 + ROWS]
        edge_s[pl.ds(k, 1)] = cot[k, 8:9]
        edge_n[pl.ds(levels + k, 1)] = 0.25 * v[k, ROWS - 1:ROWS] - 0.5 * kap[k, ROWS - 1:ROWS]
        edge_s[pl.ds(levels + k, 1)] = 0.25 * v[k, 0:1] + 0.5 * kap[k, 0:1]
        return acc

    edge_ew[...] = lax.fori_loop(0, levels, pack_level, jnp.zeros((ROWS, LANES), f32))
    edges = [
        send(edge_ew, got_ew.at[0], send_sem.at[8], edge_sem.at[0], at(1, 0)),
        send(edge_ew, got_ew.at[1], send_sem.at[9], edge_sem.at[1], at(-1, 0)),
        send(edge_n, got_s, send_sem.at[10], edge_sem.at[2], at(0, 1)),
        send(edge_s, got_n, send_sem.at[11], edge_sem.at[3], at(0, -1)),
    ]
    for edge in edges:
        edge.start()

    @pl.when(top)
    def _():
        foldz[pl.ds(z, 1)] = edge_n[...][None]

        @pl.loop(1, nz)
        def _(j):
            p = y * nz + (z + j) % nz
            send(edge_n, foldz.at[z], fold_sem.at[2], fold_sem.at[3], (p, gy)).start()

    for halo in halos:
        halo.wait_recv()
    hw, he = got2[0], got2[1]
    wide[0, 8:88] = jnp.where(lane80 < 64, he, hw)
    wide[1, 8:88] = roll_lanes(jnp.where(lane80 < 64, hw, he), 64)

    loads[6].wait()
    seam = fp_s[0] + gx * LANES + 1

    @pl.when(gy == 0)
    def _():
        plane[1, 8:16] = zero8
        wide[1, 8:16] = zero8

    first_lane, last_lane = lane80 == 0, lane80 == LANES - 1

    def neighbours(mid, beside, rows):
        return [
            jnp.where(last_lane[:rows], roll_lanes(beside, LANES - 1), roll_lanes(mid, LANES - 1)),
            jnp.where(first_lane[:rows], roll_lanes(beside, 1), roll_lanes(mid, 1)),
        ]

    def both(mid, beside):
        return neighbours(mid, beside, 80), neighbours(beside, mid, 80)

    body, up, down = pl.ds(8, 80), pl.ds(9, 80), pl.ds(7, 80)

    def least_depths():
        dm, db = plane[1, body], wide[1, body]
        (d_e, d_w), (db_e, db_w) = both(dm, db)
        for i, (a, o) in enumerate(
            [(d_e, db_e), (d_w, db_w), (plane[1, up], wide[1, up]), (plane[1, down], wide[1, down])]
        ):
            dmin[i, 0] = jnp.minimum(dm, a)
            dmin[i, 1] = jnp.minimum(db, o)

    def apply(mid_ref, beside_ref, out_ref):
        mid, beside = mid_ref[body], beside_ref[body]
        (m_e, m_w), (s_e, s_w) = both(mid, beside)
        for i, (centre, nbrs) in enumerate(
            [
                (mid, (m_e, m_w, mid_ref[up], mid_ref[down])),
                (beside, (s_e, s_w, beside_ref[up], beside_ref[down])),
            ]
        ):
            total = jnp.zeros_like(centre)
            for j in range(4):
                total = total + dmin[j, i] * (centre - nbrs[j])
            out_ref[i, body] = damping * centre + (1.0 / levels) * total

    least_depths()
    apply(plane.at[0], wide.at[0], vec1)
    apply(vec1.at[0], vec1.at[1], vec2)
    inner = pl.ds(PAD, ROWS)
    mid2 = vec2[0, inner]
    m_e, m_w = neighbours(mid2, vec2[1, inner], ROWS)
    nbrs = (m_e, m_w, vec2[0, PAD + 1:PAD + 1 + ROWS], vec2[0, PAD - 1:PAD - 1 + ROWS])
    mid3 = jnp.zeros_like(mid2)
    for j in range(4):
        mid3 = mid3 + dmin[j, 0, 8:8 + ROWS] * (mid2 - nbrs[j])
    mid3 = damping * mid2 + (1.0 / levels) * mid3
    mid0, mid1 = plane[0, inner], vec1[0, inner]

    sub8 = lax.broadcasted_iota(jnp.int32, (8, LANES), 0)
    lane8 = lax.broadcasted_iota(jnp.int32, (8, LANES), 1)

    def moment_row(fields):
        f0, f1, f2, f3 = [split(f) for f in fields]
        for j, (a, o) in enumerate([(f0, f0), (f0, f1), (f1, f1), (f1, f2), (f2, f2), (f2, f3)]):
            high, low = folded_rows(two_product(a, o))
            tot[j:j + 1] = high[0:1]
            tot[8 + j:9 + j] = low[0:1]
        tot[6:8] = jnp.zeros((2, LANES), f32)
        tot[14:16] = jnp.zeros((2, LANES), f32)
        high, low = tot[0:8], tot[8:16]
        scale = 256.0 * jnp.max(jnp.abs(high), axis=1, keepdims=True)
        coarse = (high + scale) - scale
        rest = jnp.sum((high - coarse) + low, axis=1, keepdims=True)
        high, low = renormal((jnp.sum(coarse, axis=1, keepdims=True), rest))
        row = jnp.where(lane8 == sub8, high, 0.0) + jnp.where(lane8 == sub8 + 8, low, 0.0)
        return jnp.sum(row, axis=0, keepdims=True)

    apart = top & (lax.broadcasted_iota(jnp.int32, (ROWS, LANES), 0) >= ROWS - 3)
    mom[...] = moment_row([jnp.where(apart, 0.0, f) for f in (mid0, mid1, mid2, mid3)])

    red1[pl.ds(me1, 1)] = mom[...]
    group1(lambda d: send(mom, red1.at[pl.ds(me1, 1)], red_sem.at[0], red_sem.at[1], d).start())

    for edge in edges:
        edge.wait_recv()

    @pl.when(top)
    def _():
        dmin[2, 0, 7 + ROWS:8 + ROWS] = jnp.zeros((1, LANES), f32)

    sides[...] = jnp.where((lane & 1) == 1, got_ew[1], got_ew[0])
    lane16 = lax.broadcasted_iota(jnp.int32, (16, LANES), 1)

    def level(k, carry):
        kf = k.astype(f32)
        cot[k, 7:8] = got_s[pl.ds(k, 1)]
        cot[k, 8 + ROWS:9 + ROWS] = got_n[pl.ds(k, 1)]
        qs[7:8] = got_s[pl.ds(levels + k, 1)]
        qn[8 + ROWS:9 + ROWS] = got_n[pl.ds(levels + k, 1)]
        for r in range(0, ROWS, 16):
            rows = slice(r, r + 16)
            vq, kq = 0.25 * v[k, rows], 0.5 * kap[k, rows]
            qn[8 + r:24 + r] = vq + kq
            qs[8 + r:24 + r] = vq - kq
        for r in range(0, ROWS, 16):
            rows, mid = slice(r, r + 16), slice(8 + r, 24 + r)
            ct = cot[k, mid]
            uq, kq = 0.25 * u[k, rows], 0.5 * kap[k, rows]
            qe, qw = uq + kq, uq - kq
            edge = sides[rows]
            ec = roll_lanes(edge, (LANES - 1) - 2 * k)
            eq = roll_lanes(edge, 63 - 2 * k)
            c_e = roll_lanes(jnp.where(lane16 == 0, ec, ct), LANES - 1)
            c_w = roll_lanes(jnp.where(lane16 == LANES - 1, ec, ct), 1)
            q_e = roll_lanes(jnp.where(lane16 == 0, eq, qe), LANES - 1)
            q_w = roll_lanes(jnp.where(lane16 == LANES - 1, eq, qw), 1)
            c_n, c_s = cot[k, 9 + r:25 + r], cot[k, 7 + r:23 + r]
            ke = jnp.where(dmin[0, 0, mid] > kf, time_step * (qe + q_e), 0.0)
            kw = jnp.where(dmin[1, 0, mid] > kf, time_step * (qw + q_w), 0.0)
            kn = jnp.where(dmin[2, 0, mid] > kf, time_step * (qn[8 + r:24 + r] + qn[9 + r:25 + r]), 0.0)
            ks = jnp.where(dmin[3, 0, mid] > kf, time_step * (qs[8 + r:24 + r] + qs[7 + r:23 + r]), 0.0)
            for i, face in enumerate((ke, kw, kn, ks)):
                faces[k, 1 + i, rows] = face
            faces[k, 0, rows] = ct + (ke * (c_e - ct) + kw * (ct - c_w)) + (kn * (c_n - ct) + ks * (ct - c_s))
        return carry

    lax.fori_loop(0, levels, level, 0)

    def wait_red(buf, n, sem):
        pltpu.make_async_copy(buf.at[pl.ds(0, n - 1)], buf.at[pl.ds(0, n - 1)], sem).wait()

    wait_red(red1, n1, red_sem.at[1])
    sums = red1[...]
    sums, rest = folded_rows((sums, jnp.zeros_like(sums)))
    mom2[...] = (sums + roll_lanes(rest, 8))[0:1]
    red2[pl.ds(me2, 1)] = mom2[...]
    group2(lambda d: send(mom2, red2.at[pl.ds(me2, 1)], red_sem.at[2], red_sem.at[3], d).start())

    below = sorted(range(ngy - 1), key=lambda g: -min(nx - 1 - g // nc, g // nc + 1))

    @pl.when(top)
    def _():
        pltpu.make_async_copy(foldz.at[pl.ds(0, nz - 1)], foldz.at[pl.ds(0, nz - 1)], fold_sem.at[3]).wait()
        whole = ngx * LANES
        start = (seam - LANES - gx * LANES + 2 * whole) % whole
        blk, off = start // LANES, start % LANES
        after = (blk + 1) % ngx
        fold_stage[0] = foldz[blk % nz]
        fold_stage[1] = foldz[after % nz]
        fold_y[pl.ds(y, 1)] = fold_stage[...][None]

        @pl.loop(1, ny)
        def _(j):
            p = ((y + j) % ny) * nz + z
            send(fold_stage, fold_y.at[y], fold_sem.at[4], fold_sem.at[5], (p, gy)).start()

        others = all2.at[pl.ds(0, (ngx - 1) * 16)]
        pltpu.make_async_copy(others, others, fold_sem.at[1]).wait()

        def exact_dot(a, o):
            return lax.dot(a, o, precision=lax.Precision.HIGHEST, preferred_element_type=f32)

        col = lax.broadcasted_iota(jnp.int32, (2 * LANES, LANES), 1)
        src = lax.broadcasted_iota(jnp.int32, (2 * LANES, LANES), 0)
        pick = (src == off + (LANES - 1) - col).astype(f32)
        block = lax.broadcasted_iota(jnp.int32, (ngx, ngx), 0)
        source = lax.broadcasted_iota(jnp.int32, (ngx, ngx), 1)
        order = ((block + source - blk - gx + 2 * ngx) % ngx == 0).astype(f32)
        fields = [[all2[pl.ds(8 * f + q, ngx, stride=16)] for q in range(2, 8)] for f in range(2)]
        mirror = [fields[f][q] for f in range(2) for q in (5, 4, 3)]
        turned = exact_dot(order, jnp.concatenate(mirror, axis=1))
        turned = [turned[:, i * LANES:(i + 1) * LANES] for i in range(6)]
        turned = [jnp.concatenate([t, pltpu.roll(t, 1, 0)], axis=1) for t in turned]
        mir[...] = exact_dot(jnp.concatenate(turned, axis=0), pick)
        mirror = [mir[i * ngx:(i + 1) * ngx] for i in range(6)]
        values, depth = fields[0] + mirror[:3], fields[1] + mirror[3:]
        spot = lax.broadcasted_iota(jnp.int32, (ngx, LANES), 1)

        def beside(t):
            ahead, behind = roll_lanes(t, LANES - 1), roll_lanes(t, 1)
            return (
                jnp.where(spot == LANES - 1, pltpu.roll(ahead, ngx - 1, 0), ahead),
                jnp.where(spot == 0, pltpu.roll(behind, 1, 0), behind),
            )

        least = {
            i: [jnp.minimum(depth[i], t) for t in (*beside(depth[i]), depth[i + 1], depth[i - 1])]
            for i in range(1, 8)
        }

        def step(f, rows):
            out = {}
            for i in rows:
                total = jnp.zeros_like(f[i])
                for d, t in zip(least[i], (*beside(f[i]), f[i + 1], f[i - 1])):
                    total = total + d * (f[i] - t)
                out[i] = damping * f[i] + (1.0 / levels) * total
            return out

        band1 = step(values, range(1, 8))
        band2 = step(band1, range(2, 7))
        band3 = step(band2, range(3, 6))
        band[...] = moment_row(
            [jnp.concatenate([f[i] for i in (3, 4, 5)], axis=0) for f in (values, band1, band2, band3)]
        )
        red2[n2:n2 + 1] = band[...]
        for g in below:
            send(band, red2.at[pl.ds(n2, 1)], band_sem.at[0], band_sem.at[1], (gx, g)).start()

        for i in range(6):
            f, row = i // 3, PAD + ROWS + i % 3
            mine, ahead, behind = [mir[pl.ds(i * ngx + (gx + d) % ngx, 1)] for d in (0, 1, ngx - 1)]
            plane[f, row:row + 1] = mine
            wide[f, row:row + 1] = jnp.where(lane8[0:1] < 64, ahead, behind)
        least_depths()
        apply(plane.at[0], wide.at[0], vec1)
        apply(vec1.at[0], vec1.at[1], vec2)

        pltpu.make_async_copy(fold_y.at[pl.ds(0, ny - 1)], fold_y.at[pl.ds(0, ny - 1)], fold_sem.at[5]).wait()
        got_n[...] = exact_dot(jnp.concatenate([fold_y[blk // nz, 0], fold_y[after // nz, 1]], axis=1), pick)
        here = slice(ROWS - 1, ROWS)

        def across(k, carry):
            ct = cot[k, 7 + ROWS:8 + ROWS]
            half = 0.25 * v[k, here] + 0.5 * kap[k, here] - got_n[pl.ds(levels + k, 1)]
            kn = jnp.where(dmin[2, 0, 7 + ROWS:8 + ROWS] > k.astype(f32), time_step * half, 0.0)
            faces[k, 3, here] = kn
            faces[k, 0, here] += kn * (got_n[pl.ds(k, 1)] - ct)
            return carry

        lax.fori_loop(0, levels, across, 0)

    store = pltpu.make_async_copy(faces, faces_h, store_sem.at[0])
    store.start()

    wait_red(red2, n2, red_sem.at[3])

    @pl.when(gy != ngy - 1)
    def _():
        one = red2.at[pl.ds(n2, 1)]
        pltpu.make_async_copy(one, one, band_sem.at[1]).wait()

    sums = red2[...]
    sums, rest = folded_rows((sums, jnp.zeros_like(sums)))
    rest = rest + pltpu.roll(sums, LANES - 8, 1)
    parts = []
    for part in (sums, rest):
        part = jnp.sum(jnp.where(lane8 == sub8, part, 0.0), axis=1, keepdims=True)
        parts.append(jnp.broadcast_to(part, (8, LANES)))
    tot[0:8], tot[8:16] = renormal(parts)
    pairs = [[jnp.broadcast_to(tot[i:i + 1], (8, LANES)) for i in (j, 8 + j)] for j in range(6)]
    m = [high for high, low in pairs]
    lo, hi = 0.0999, 8.2
    rho = m[1] / m[0]
    rho_parts = split(rho)

    def centred(a, o):
        p, rest = two_product(rho_parts, split(o[0]))
        return renormal(pair_add(a, (-p, -(rest + rho * o[1]))))

    s1 = [centred(pairs[j + 1], pairs[j]) for j in range(5)]
    n = [centred(s1[j + 1], s1[j])[0] for j in range(4)]
    n[0] = jnp.maximum(n[0], 0.0)

    def bounded(t, least, most):
        return jnp.where(t >= least, jnp.minimum(t, most), least)

    e1 = n[0] / m[0]
    rho1 = bounded(n[1] / n[0], lo, hi)
    p1 = bounded(rho1 - e1 / rho, lo, hi)
    k0 = n[2] - rho1 * n[1] - e1 * n[0]
    k1 = n[3] - 2.0 * rho1 * n[2] + rho1 * rho1 * n[1] - 2.0 * e1 * rho * n[0] + e1 * e1 * m[1]
    e2 = bounded(k0 / n[0], 0.0, 70.0)
    rho2 = bounded(k1 / k0, lo, hi)
    p2 = bounded(rho2 - e2 / p1, lo, hi)
    z0 = 1.0 / rho
    z1 = -z0 / p1
    y2 = -z1 / p2
    y1 = z1 - e2 / p1 * y2
    y0 = z0 - e1 / rho * y1
    a0 = y0 - rho * y1 + (rho1 * rho - e1) * y2
    a1 = y1 - (rho + rho1) * y2

    def spread(a, rows):
        return jnp.broadcast_to(a[0:1], (rows, LANES))

    rows80 = [spread(a, 80) for a in (a0, a1, y2)]
    h_mid = rows80[0] * plane[0, body] + rows80[1] * vec1[0, body] + rows80[2] * vec2[0, body]
    h_side = rows80[0] * wide[0, body] + rows80[1] * vec1[1, body] + rows80[2] * vec2[1, body]
    hv[0, body] = h_mid
    inner_mid, inner_side = h_mid[8:8 + ROWS], h_side[8:8 + ROWS]
    h_e, h_w = neighbours(inner_mid, inner_side, ROWS)
    hv[1, inner] = h_e - inner_mid
    hv[2, inner] = inner_mid - h_w
    hv[3, inner] = hv[0, PAD + 1:PAD + 1 + ROWS] - inner_mid
    hv[4, inner] = inner_mid - hv[0, PAD - 1:PAD - 1 + ROWS]
    hv[5, inner] = plane[1, inner]
    height = pltpu.make_async_copy(hv.at[:, inner], height_h, store_sem.at[1])
    height.start()

    for halo in halos:
        halo.wait_send()
    for edge in edges:
        edge.wait_send()
    wait_red(red1, n1, red_sem.at[0])
    wait_red(red2, n2, red_sem.at[2])

    @pl.when(top)
    def _():
        others = all2.at[pl.ds(0, (ngx - 1) * 16)]
        pltpu.make_async_copy(others, others, fold_sem.at[0]).wait()
        some = red2.at[pl.ds(0, ngy - 1)]
        pltpu.make_async_copy(some, some, band_sem.at[0]).wait()
        pltpu.make_async_copy(foldz.at[pl.ds(0, nz - 1)], foldz.at[pl.ds(0, nz - 1)], fold_sem.at[2]).wait()
        pltpu.make_async_copy(fold_y.at[pl.ds(0, ny - 1)], fold_y.at[pl.ds(0, ny - 1)], fold_sem.at[4]).wait()

    height.wait()
    store.wait()


def finish(levels, group, faces_h, height_h, th_h, out_h, hadj_h, th, faces, height, out, sem):
    parts = [pl.ds(k, group) for k in range(0, levels, group)]
    first = [
        pltpu.make_async_copy(height_h, height, sem.at[0]),
        pltpu.make_async_copy(th_h, th, sem.at[1]),
    ]
    loads = [
        pltpu.make_async_copy(faces_h.at[p], faces.at[p], sem.at[2 + i]) for i, p in enumerate(parts)
    ]
    for load in first + loads:
        load.start()
    first[0].wait()
    stores = [pltpu.make_async_copy(height.at[0], hadj_h, sem.at[0])]
    stores[0].start()
    first[1].wait()
    for i, p in enumerate(parts):
        loads[i].wait()
        for r in range(0, ROWS, 8):
            rows = slice(r, r + 8)
            hc, de, dw, dn, ds_, wet = [height[j, rows] for j in range(6)]
            for k in range(i * group, (i + 1) * group):
                grown = (
                    jnp.where(wet > float(k), hc, 0.0)
                    + (faces[k, 1, rows] * de + faces[k, 2, rows] * dw)
                    + (faces[k, 3, rows] * dn + faces[k, 4, rows] * ds_)
                )
                out[k, rows] = faces[k, 0, rows] + th[k] * grown
        stores.append(pltpu.make_async_copy(out.at[p], out_h.at[p], sem.at[2 + i]))
        stores[-1].start()
    for store in stores:
        store.wait()


def solution(mesh):
    ngx, ngy = mesh.shape["gx"], mesh.shape["gy"]
    nc = 2
    nx = ngy // nc
    ny = 4 if ngx == 32 else 2
    nz = ngx // ny

    def local(cot, b, u, v, kap, th, dep, fp):
        levels = cot.shape[0]
        f32 = jnp.float32

        def vmem(*shape, dtype=f32):
            return pltpu.VMEM(shape, dtype)

        cube = (levels, ROWS, LANES)
        scratch = [
            pltpu.SMEM((LANES,), jnp.int32),
            vmem(levels, 80, LANES), vmem(*cube), vmem(*cube), vmem(*cube),
            vmem(ROWS, LANES, dtype=jnp.int32),
            vmem(2, 96, LANES), vmem(2, 96, LANES),
            vmem(ROWS, LANES), vmem(2, 80, LANES), vmem(4, 2, 80, LANES),
            vmem(2, 96, LANES), vmem(2, 96, LANES),
            vmem(ROWS, LANES), vmem(2, ROWS, LANES),
            vmem(FOLD, LANES), vmem(FOLD, LANES), vmem(FOLD, LANES), vmem(FOLD, LANES),
            vmem(16, LANES), vmem(ngx * 16, LANES), vmem(ngx * 6, LANES),
            vmem(nz, FOLD, LANES), vmem(2, FOLD, LANES), vmem(ny, 2, FOLD, LANES),
            vmem(ROWS, LANES),
            vmem(80, LANES), vmem(80, LANES),
            vmem(levels, 5, ROWS, LANES), vmem(6, 96, LANES),
            vmem(1, LANES), vmem(max(8, nz * nc), LANES), vmem(1, LANES), vmem(8 if nx * ny < 8 else 32, LANES), vmem(1, LANES), vmem(16, LANES),
            pltpu.SemaphoreType.DMA((7,)), pltpu.SemaphoreType.DMA((2,)),
            pltpu.SemaphoreType.DMA((12,)), pltpu.SemaphoreType.DMA((8,)),
            pltpu.SemaphoreType.DMA((4,)), pltpu.SemaphoreType.DMA((4,)),
            pltpu.SemaphoreType.DMA((6,)), pltpu.SemaphoreType.DMA((2,)),
        ]
        hbm = pl.BlockSpec(memory_space=pltpu.HBM)
        limit = 62 * 1024 * 1024
        faces, height = pl.pallas_call(
            functools.partial(kernel, nz, ny, nc, nx, levels),
            out_shape=(
                jax.ShapeDtypeStruct((levels, 5, ROWS, LANES), f32),
                jax.ShapeDtypeStruct((6, ROWS, LANES), f32),
            ),
            in_specs=[hbm] * 7,
            out_specs=(hbm, hbm),
            scratch_shapes=scratch,
            compiler_params=pltpu.CompilerParams(
                collective_id=0, has_side_effects=True, vmem_limit_bytes=limit
            ),
        )(cot, b, u, v, kap, dep, fp)
        group = 5 if levels % 5 == 0 else 1
        return pl.pallas_call(
            functools.partial(finish, levels, group),
            out_shape=(jax.ShapeDtypeStruct(cube, f32), jax.ShapeDtypeStruct((ROWS, LANES), f32)),
            in_specs=[hbm] * 3,
            out_specs=(hbm, hbm),
            scratch_shapes=[
                pltpu.SMEM((levels,), f32), vmem(levels, 5, ROWS, LANES), vmem(6, ROWS, LANES), vmem(*cube),
                pltpu.SemaphoreType.DMA((2 + levels // group,)),
            ],
            compiler_params=pltpu.CompilerParams(vmem_limit_bytes=limit),
        )(faces, height, th)

    in_specs = (
        P(None, "gy", "gx"), P("gy", "gx"), P(None, "gy", "gx"), P(None, "gy", "gx"),
        P(None, "gy", "gx"), P(), P("gy", "gx"), P("gx"),
    )
    out_specs = (P(None, "gy", "gx"), P("gy", "gx"))
    return jax.shard_map(local, mesh=mesh, in_specs=in_specs, out_specs=out_specs, check_vma=False)
```

time: 40.8 us -> 31.9 us (0.78)
  local copies, waits for them, and re-layouts: 8.9 us -> 0 us
    unnamed x18 -> x0, local copies, waits for them, and re-layouts: 8.9 us -> none
    pallas_call x0 -> x1, Pallas kernels: none -> 3.06 us  [local(): pl.pallas_call(functools.partial(finish, levels, group), out_shape=(jax.S...]
    pallas_call x1, Pallas kernels: 30.8 us -> 28.2 us  [local(): pl.pallas_call(functools.partial(kernel, nz, ny, nc, nx, levels), out_sha...]
where the time goes in v2:
time: 31.9 us
  Pallas kernels  31.2 us (98%)
  between operations  0.64 us (2%)
    pallas_call x1, Pallas kernels, local(): pl.pallas_call(functools.partial(kernel, nz, ny, nc, nx, levels), out_sha...  28.2 us
    pallas_call x1, Pallas kernels, local(): pl.pallas_call(functools.partial(finish, levels, group), out_shape=(jax.S...  3.06 us

profile of v2, /device:TPU:1, one launch (start us, length us, event | category | flops | bytes accessed | tf_op | source)
XLA Modules:
  0.0 31.9 jit_solution(4276168154077527658)
XLA Ops:
  0.6 28.2 %shard_map.95 = (f32[25,5,64,128]{3,2,1,0:T(8,128)}, f32[6,64,128]{2,1,0:T(8,128)}) custom-call(f32[25,64,128]{2,1,0:T(8,128)} %cot_h.1, f32[64,128]{1,0:T(8,128)} %b_h.1, f32[25,64,128]{2,1,0:T(8,128)} %u_h.1, f32[25,64,128]{2,1,0:T(8,128)} %v_h.1, f32[25,64,128]{2,1,0:T(8,128)} %k_h.1, s32[64,128]{1,0:T(8,128)} %dep_h.1, s32[128]{0:T(128)} %fp_h.1), custom_call_target="tpu_custom_call" | custom-call | tf_op jit(solution)/shard_map/pallas_call | solution.py:630
  28.8 3.1 %shard_map.96 = (f32[25,64,128]{2,1,0:T(8,128)}, f32[64,128]{1,0:T(8,128)}) custom-call(f32[25,5,64,128]{3,2,1,0:T(8,128)} %get-tuple-element.4.faces_h, f32[6,64,128]{2,1,0:T(8,128)} %get-tuple-element.5.height_h, f32[25]{0:T(128)} %th_h.1), custom_call_target="tpu_custom_call" | custom-call | tf_op jit(solution)/shard_map/pallas_call | solution.py:644

commit v3 on v2

--- a/solution.py
+++ b/solution.py
@@ -68,7 +68,7 @@
     top2, all2, mir, foldz, fold_stage, fold_y, sides,
     qn, qs, faces, hv,
     mom, red1, mom2, red2, band, tot,
-    load_sem, store_sem, send_sem, halo_sem, edge_sem, red_sem, fold_sem, band_sem,
+    load_sem, store_sem, send_sem, halo_sem, edge_sem, red_sem, fold_sem, band_sem, ready_sem,
 ):
     gx, gy = lax.axis_index("gx"), lax.axis_index("gy")
     ngx, ngy = ny * nz, nx * nc
@@ -104,6 +104,9 @@
         return sorted(range(n), key=lambda d: (-min(d, n - d), d))
 
     far_y = [((y + d) % ny) * nz for d in far_first(ny)]
+    def ready(device):
+        pl.semaphore_signal(ready_sem, inc=1, device_id=device, device_id_type=MESH)
+
     n1, n2 = nz * nc, nx * ny
     me1, me2 = z * nc + c, y * nx + x
     far_z = [(z + d) % nz for d in far_first(nz)]
@@ -134,14 +137,6 @@
         greet(at(*d))
     group1(greet)
     group2(greet)
-
-    @pl.when(top)
-    def _():
-        everyone_on_top(greet)
-
-    @pl.when(gy != ngy - 1)
-    def _():
-        greet((gx, ngy - 1))
 
     zero8 = jnp.zeros((8, LANES), f32)
     for part, n in ((red1, n1), (red2, n2 + 1)):
@@ -159,7 +154,7 @@
         (lane < 32) | (lane >= 96), plane[0, PAD:PAD + ROWS], roll_lanes(depth_f, 64)
     )
 
-    pl.semaphore_wait(barrier, 8 + n1 - 1 + n2 - 1 + jnp.where(top, ngx - 1 + ngy - 1, 0))
+    pl.semaphore_wait(barrier, 8 + n1 - 1 + n2 - 1)
 
     def send(src, dst, sem_out, sem_in, device):
         copy = pltpu.make_async_remote_copy(
@@ -185,16 +180,19 @@
                 src, dst = pack2.at[pl.ds(0, 8)], got2.at[side, pl.ds(ROWS + 8, 8)]
         halos.append(send(src, dst, send_sem.at[i], halo_sem.at[i], at(dx, dy)))
 
-    @pl.when(top)
-    def _():
-        top2[0:8] = plane[0, last]
-        top2[8:16] = plane[1, last]
-        mine = pl.ds(pl.multiple_of(gx * 16, 16), 16)
-        all2[mine] = top2[...]
-        everyone_on_top(lambda d: send(top2, all2.at[mine], fold_sem.at[0], fold_sem.at[1], d).start())
-
     for halo in halos:
         halo.start()
+
+    @pl.when(c == nc - 1)
+    def _():
+        @pl.when(top)
+        def _():
+            for d in range(1, ny):
+                ready(((y + d) % ny * nz + z, gy))
+
+        @pl.when(x < nx - 1)
+        def _():
+            ready((gx, ngy - 1))
 
     for load in loads[2:6]:
         load.wait()
@@ -225,6 +223,13 @@
 
     @pl.when(top)
     def _():
+        pl.semaphore_wait(ready_sem, ny - 1 + nx - 1)
+        top2[0:8] = plane[0, last]
+        top2[8:16] = plane[1, last]
+        mine = pl.ds(pl.multiple_of(gx * 16, 16), 16)
+        all2[mine] = top2[...]
+        everyone_on_top(lambda d: send(top2, all2.at[mine], fold_sem.at[0], fold_sem.at[1], d).start())
+
         foldz[pl.ds(z, 1)] = edge_n[...][None]
 
         @pl.loop(1, nz)
@@ -624,6 +629,7 @@
             pltpu.SemaphoreType.DMA((12,)), pltpu.SemaphoreType.DMA((8,)),
             pltpu.SemaphoreType.DMA((4,)), pltpu.SemaphoreType.DMA((4,)),
             pltpu.SemaphoreType.DMA((6,)), pltpu.SemaphoreType.DMA((2,)),
+            pltpu.SemaphoreType.REGULAR,
         ]
         hbm = pl.BlockSpec(memory_space=pltpu.HBM)
         limit = 62 * 1024 * 1024

time: 31.9 us -> 31.1 us (0.975); the launches traced: 31.9 us -> 30.6 us
  Pallas kernels: 31.2 us -> 29.9 us
    pallas_call x1, Pallas kernels: 28.2 us -> 26.9 us  [local(): pl.pallas_call(functools.partial(kernel, nz, ny, nc, nx, levels), out_sha...]
where the time goes in v3:
time: 31.1 us; the launch traced here: 30.6 us
  Pallas kernels  29.9 us (96%)
  between operations  0.64 us (2%)
    pallas_call x1, Pallas kernels, local(): pl.pallas_call(functools.partial(kernel, nz, ny, nc, nx, levels), out_sha...  26.9 us
    pallas_call x1, Pallas kernels, local(): pl.pallas_call(functools.partial(finish, levels, group), out_shape=(jax.S...  3.06 us

profile of v3, /device:TPU:1, one launch (start us, length us, event | category | flops | bytes accessed | tf_op | source)
XLA Modules:
  0.0 30.6 jit_solution(9012673883490638899)
XLA Ops:
  0.6 26.9 %shard_map.95 = (f32[25,5,64,128]{3,2,1,0:T(8,128)}, f32[6,64,128]{2,1,0:T(8,128)}) custom-call(f32[25,64,128]{2,1,0:T(8,128)} %cot_h.1, f32[64,128]{1,0:T(8,128)} %b_h.1, f32[25,64,128]{2,1,0:T(8,128)} %u_h.1, f32[25,64,128]{2,1,0:T(8,128)} %v_h.1, f32[25,64,128]{2,1,0:T(8,128)} %k_h.1, s32[64,128]{1,0:T(8,128)} %dep_h.1, s32[128]{0:T(128)} %fp_h.1), custom_call_target="tpu_custom_call" | custom-call | tf_op jit(solution)/shard_map/pallas_call | solution.py:636
  27.5 3.1 %shard_map.96 = (f32[25,64,128]{2,1,0:T(8,128)}, f32[64,128]{1,0:T(8,128)}) custom-call(f32[25,5,64,128]{3,2,1,0:T(8,128)} %get-tuple-element.4.faces_h, f32[6,64,128]{2,1,0:T(8,128)} %get-tuple-element.5.height_h, f32[25]{0:T(128)} %th_h.1), custom_call_target="tpu_custom_call" | custom-call | tf_op jit(solution)/shard_map/pallas_call | solution.py:650

commit v4 on v3

--- a/solution.py
+++ b/solution.py
@@ -61,12 +61,12 @@
 
 
 def kernel(
-    nz, ny, nc, nx, levels,
-    cot_h, b_h, u_h, v_h, k_h, dep_h, fp_h, faces_h, height_h,
-    fp_s, cot, u, v, kap, dint, plane, wide, pack2, got2, dmin, vec1, vec2,
+    nz, ny, nc, nx, levels, group,
+    cot_h, b_h, u_h, v_h, k_h, th_h, dep_h, fp_h, out_h, hadj_h,
+    th_s, fp_s, cot, u, v, kap, dint, plane, wide, pack2, got2, dmin, vec1, vec2,
     edge_ew, got_ew, edge_n, edge_s, got_n, got_s,
     top2, all2, mir, foldz, fold_stage, fold_y, sides,
-    qn, qs, faces, hv,
+    qn, qs, faces, hv, outv,
     mom, red1, mom2, red2, band, tot,
     load_sem, store_sem, send_sem, halo_sem, edge_sem, red_sem, fold_sem, band_sem, ready_sem,
 ):
@@ -91,6 +91,7 @@
         pltpu.make_async_copy(k_h, kap, load_sem.at[4]),
         pltpu.make_async_copy(v_h, v, load_sem.at[5]),
         pltpu.make_async_copy(fp_h, fp_s, load_sem.at[6]),
+        pltpu.make_async_copy(th_h, th_s, load_sem.at[7]),
     ]
     for load in loads:
         load.start()
@@ -200,18 +201,19 @@
     edge_n[2 * levels:FOLD] = jnp.zeros((FOLD - 2 * levels, LANES), f32)
     edge_s[2 * levels:FOLD] = jnp.zeros((FOLD - 2 * levels, LANES), f32)
 
-    def pack_level(k, acc):
-        face = 0.25 * u[k] + half * kap[k]
+    def pack_levels(g, acc):
         place = lane >> 1
-        acc = jnp.where(place == k, roll_lanes(cot[k, 8:8 + ROWS], 2 * k + 1), acc)
-        acc = jnp.where(place == k + 32, roll_lanes(face, 2 * k + 65), acc)
-        edge_n[pl.ds(k, 1)] = cot[k, 7 + ROWS:8 + ROWS]
-        edge_s[pl.ds(k, 1)] = cot[k, 8:9]
-        edge_n[pl.ds(levels + k, 1)] = 0.25 * v[k, ROWS - 1:ROWS] - 0.5 * kap[k, ROWS - 1:ROWS]
-        edge_s[pl.ds(levels + k, 1)] = 0.25 * v[k, 0:1] + 0.5 * kap[k, 0:1]
+        for k in [g * group + j for j in range(group)]:
+            face = 0.25 * u[k] + half * kap[k]
+            acc = jnp.where(place == k, roll_lanes(cot[k, 8:8 + ROWS], 2 * k + 1), acc)
+            acc = jnp.where(place == k + 32, roll_lanes(face, 2 * k + 65), acc)
+            edge_n[pl.ds(k, 1)] = cot[k, 7 + ROWS:8 + ROWS]
+            edge_s[pl.ds(k, 1)] = cot[k, 8:9]
+            edge_n[pl.ds(levels + k, 1)] = 0.25 * v[k, ROWS - 1:ROWS] - 0.5 * kap[k, ROWS - 1:ROWS]
+            edge_s[pl.ds(levels + k, 1)] = 0.25 * v[k, 0:1] + 0.5 * kap[k, 0:1]
         return acc
 
-    edge_ew[...] = lax.fori_loop(0, levels, pack_level, jnp.zeros((ROWS, LANES), f32))
+    edge_ew[...] = lax.fori_loop(0, levels // group, pack_levels, jnp.zeros((ROWS, LANES), f32))
     edges = [
         send(edge_ew, got_ew.at[0], send_sem.at[8], edge_sem.at[0], at(1, 0)),
         send(edge_ew, got_ew.at[1], send_sem.at[9], edge_sem.at[1], at(-1, 0)),
@@ -328,47 +330,47 @@
     for edge in edges:
         edge.wait_recv()
 
-    @pl.when(top)
-    def _():
-        dmin[2, 0, 7 + ROWS:8 + ROWS] = jnp.zeros((1, LANES), f32)
-
     sides[...] = jnp.where((lane & 1) == 1, got_ew[1], got_ew[0])
     lane16 = lax.broadcasted_iota(jnp.int32, (16, LANES), 1)
 
-    def level(k, carry):
-        kf = k.astype(f32)
-        cot[k, 7:8] = got_s[pl.ds(k, 1)]
-        cot[k, 8 + ROWS:9 + ROWS] = got_n[pl.ds(k, 1)]
-        qs[7:8] = got_s[pl.ds(levels + k, 1)]
-        qn[8 + ROWS:9 + ROWS] = got_n[pl.ds(levels + k, 1)]
-        for r in range(0, ROWS, 16):
-            rows = slice(r, r + 16)
-            vq, kq = 0.25 * v[k, rows], 0.5 * kap[k, rows]
-            qn[8 + r:24 + r] = vq + kq
-            qs[8 + r:24 + r] = vq - kq
-        for r in range(0, ROWS, 16):
-            rows, mid = slice(r, r + 16), slice(8 + r, 24 + r)
-            ct = cot[k, mid]
-            uq, kq = 0.25 * u[k, rows], 0.5 * kap[k, rows]
-            qe, qw = uq + kq, uq - kq
-            edge = sides[rows]
-            ec = roll_lanes(edge, (LANES - 1) - 2 * k)
-            eq = roll_lanes(edge, 63 - 2 * k)
-            c_e = roll_lanes(jnp.where(lane16 == 0, ec, ct), LANES - 1)
-            c_w = roll_lanes(jnp.where(lane16 == LANES - 1, ec, ct), 1)
-            q_e = roll_lanes(jnp.where(lane16 == 0, eq, qe), LANES - 1)
-            q_w = roll_lanes(jnp.where(lane16 == LANES - 1, eq, qw), 1)
-            c_n, c_s = cot[k, 9 + r:25 + r], cot[k, 7 + r:23 + r]
-            ke = jnp.where(dmin[0, 0, mid] > kf, time_step * (qe + q_e), 0.0)
-            kw = jnp.where(dmin[1, 0, mid] > kf, time_step * (qw + q_w), 0.0)
-            kn = jnp.where(dmin[2, 0, mid] > kf, time_step * (qn[8 + r:24 + r] + qn[9 + r:25 + r]), 0.0)
-            ks = jnp.where(dmin[3, 0, mid] > kf, time_step * (qs[8 + r:24 + r] + qs[7 + r:23 + r]), 0.0)
-            for i, face in enumerate((ke, kw, kn, ks)):
-                faces[k, 1 + i, rows] = face
-            faces[k, 0, rows] = ct + (ke * (c_e - ct) + kw * (ct - c_w)) + (kn * (c_n - ct) + ks * (ct - c_s))
+    def level_group(begin, end, g, carry):
+        ks = [g * group + j for j in range(group)]
+        for j, k in enumerate(ks):
+            cot[k, 7:8] = got_s[pl.ds(k, 1)]
+            cot[k, 8 + ROWS:9 + ROWS] = got_n[pl.ds(k, 1)]
+            qs[j, 7:8] = got_s[pl.ds(levels + k, 1)]
+            qn[j, 8 + ROWS:9 + ROWS] = got_n[pl.ds(levels + k, 1)]
+            for r in range(max(begin - 8, 0), min(end + 8, ROWS), 8):
+                rows = slice(r, r + 8)
+                vq, kq = 0.25 * v[k, rows], 0.5 * kap[k, rows]
+                qn[j, 8 + r:16 + r] = vq + kq
+                qs[j, 8 + r:16 + r] = vq - kq
+        for r in range(begin, end, 16):
+            for j, k in enumerate(ks):
+                kf = k.astype(f32)
+                rows, mid = slice(r, r + 16), slice(8 + r, 24 + r)
+                ct = cot[k, mid]
+                uq, kq = 0.25 * u[k, rows], 0.5 * kap[k, rows]
+                qe, qw = uq + kq, uq - kq
+                edge = sides[rows]
+                ec = roll_lanes(edge, (LANES - 1) - 2 * k)
+                eq = roll_lanes(edge, 63 - 2 * k)
+                c_e = roll_lanes(jnp.where(lane16 == 0, ec, ct), LANES - 1)
+                c_w = roll_lanes(jnp.where(lane16 == LANES - 1, ec, ct), 1)
+                q_e = roll_lanes(jnp.where(lane16 == 0, eq, qe), LANES - 1)
+                q_w = roll_lanes(jnp.where(lane16 == LANES - 1, eq, qw), 1)
+                c_n, c_s = cot[k, 9 + r:25 + r], cot[k, 7 + r:23 + r]
+                ke = jnp.where(dmin[0, 0, mid] > kf, time_step * (qe + q_e), 0.0)
+                kw = jnp.where(dmin[1, 0, mid] > kf, time_step * (qw + q_w), 0.0)
+                kn = jnp.where(dmin[2, 0, mid] > kf, time_step * (qn[j, mid] + qn[j, 9 + r:25 + r]), 0.0)
+                ks_ = jnp.where(dmin[3, 0, mid] > kf, time_step * (qs[j, mid] + qs[j, 7 + r:23 + r]), 0.0)
+                for i, face in enumerate((ke, kw, kn, ks_)):
+                    faces[k, 1 + i, rows] = face
+                faces[k, 0, rows] = ct + (ke * (c_e - ct) + kw * (ct - c_w)) + (kn * (c_n - ct) + ks_ * (ct - c_s))
         return carry
 
-    lax.fori_loop(0, levels, level, 0)
+    cut = 48
+    lax.fori_loop(0, levels // group, functools.partial(level_group, 0, cut), 0)
 
     def wait_red(buf, n, sem):
         pltpu.make_async_copy(buf.at[pl.ds(0, n - 1)], buf.at[pl.ds(0, n - 1)], sem).wait()
@@ -384,11 +386,12 @@
 
     @pl.when(top)
     def _():
-        pltpu.make_async_copy(foldz.at[pl.ds(0, nz - 1)], foldz.at[pl.ds(0, nz - 1)], fold_sem.at[3]).wait()
         whole = ngx * LANES
         start = (seam - LANES - gx * LANES + 2 * whole) % whole
         blk, off = start // LANES, start % LANES
         after = (blk + 1) % ngx
+
+        pltpu.make_async_copy(foldz.at[pl.ds(0, nz - 1)], foldz.at[pl.ds(0, nz - 1)], fold_sem.at[3]).wait()
         fold_stage[0] = foldz[blk % nz]
         fold_stage[1] = foldz[after % nz]
         fold_y[pl.ds(y, 1)] = fold_stage[...][None]
@@ -461,21 +464,12 @@
         apply(vec1.at[0], vec1.at[1], vec2)
 
         pltpu.make_async_copy(fold_y.at[pl.ds(0, ny - 1)], fold_y.at[pl.ds(0, ny - 1)], fold_sem.at[5]).wait()
-        got_n[...] = exact_dot(jnp.concatenate([fold_y[blk // nz, 0], fold_y[after // nz, 1]], axis=1), pick)
-        here = slice(ROWS - 1, ROWS)
-
-        def across(k, carry):
-            ct = cot[k, 7 + ROWS:8 + ROWS]
-            half = 0.25 * v[k, here] + 0.5 * kap[k, here] - got_n[pl.ds(levels + k, 1)]
-            kn = jnp.where(dmin[2, 0, 7 + ROWS:8 + ROWS] > k.astype(f32), time_step * half, 0.0)
-            faces[k, 3, here] = kn
-            faces[k, 0, here] += kn * (got_n[pl.ds(k, 1)] - ct)
-            return carry
-
-        lax.fori_loop(0, levels, across, 0)
-
-    store = pltpu.make_async_copy(faces, faces_h, store_sem.at[0])
-    store.start()
+        got = exact_dot(jnp.concatenate([fold_y[blk // nz, 0], fold_y[after // nz, 1]], axis=1), pick)
+        row = lax.broadcasted_iota(jnp.int32, (FOLD, LANES), 0)
+        got_n[...] = jnp.where(row < levels, got, -got)
+
+    lax.fori_loop(0, levels // group, functools.partial(level_group, cut, ROWS), 0)
+    loads[7].wait()
 
     wait_red(red2, n2, red_sem.at[3])
 
@@ -539,8 +533,28 @@
     hv[3, inner] = hv[0, PAD + 1:PAD + 1 + ROWS] - inner_mid
     hv[4, inner] = inner_mid - hv[0, PAD - 1:PAD - 1 + ROWS]
     hv[5, inner] = plane[1, inner]
-    height = pltpu.make_async_copy(hv.at[:, inner], height_h, store_sem.at[1])
+    height = pltpu.make_async_copy(hv.at[0, inner], hadj_h, load_sem.at[0])
     height.start()
+
+    def store_of(g):
+        part = pl.ds(g * group, group)
+        return pltpu.make_async_copy(outv.at[part], out_h.at[part], store_sem.at[g])
+
+    def finish_levels(g, carry):
+        for r in range(0, ROWS, 8):
+            rows = slice(r, r + 8)
+            hc, de, dw, dn, ds_, wet = [hv[i, PAD + r:PAD + r + 8] for i in range(6)]
+            for k in [g * group + j for j in range(group)]:
+                grown = (
+                    jnp.where(wet > k.astype(f32), hc, 0.0)
+                    + (faces[k, 1, rows] * de + faces[k, 2, rows] * dw)
+                    + (faces[k, 3, rows] * dn + faces[k, 4, rows] * ds_)
+                )
+                outv[k, rows] = faces[k, 0, rows] + th_s[k] * grown
+        store_of(g).start()
+        return carry
+
+    lax.fori_loop(0, levels // group, finish_levels, 0)
 
     for halo in halos:
         halo.wait_send()
@@ -559,38 +573,22 @@
         pltpu.make_async_copy(fold_y.at[pl.ds(0, ny - 1)], fold_y.at[pl.ds(0, ny - 1)], fold_sem.at[4]).wait()
 
     height.wait()
-    store.wait()
-
-
-def finish(levels, group, faces_h, height_h, th_h, out_h, hadj_h, th, faces, height, out, sem):
+    for g in range(levels // group):
+        store_of(g).wait()
+
+
+def hand_on(levels, group, from_h, hfrom_h, out_h, hout_h, held, hheld, sem_in, sem_out):
     parts = [pl.ds(k, group) for k in range(0, levels, group)]
-    first = [
-        pltpu.make_async_copy(height_h, height, sem.at[0]),
-        pltpu.make_async_copy(th_h, th, sem.at[1]),
-    ]
-    loads = [
-        pltpu.make_async_copy(faces_h.at[p], faces.at[p], sem.at[2 + i]) for i, p in enumerate(parts)
-    ]
-    for load in first + loads:
+    last = len(parts)
+    loads = [pltpu.make_async_copy(from_h.at[p], held.at[p], sem_in.at[i]) for i, p in enumerate(parts)]
+    loads.append(pltpu.make_async_copy(hfrom_h, hheld, sem_in.at[last]))
+    stores = [pltpu.make_async_copy(held.at[p], out_h.at[p], sem_out.at[i]) for i, p in enumerate(parts)]
+    stores.append(pltpu.make_async_copy(hheld, hout_h, sem_out.at[last]))
+    for load in loads:
         load.start()
-    first[0].wait()
-    stores = [pltpu.make_async_copy(height.at[0], hadj_h, sem.at[0])]
-    stores[0].start()
-    first[1].wait()
-    for i, p in enumerate(parts):
-        loads[i].wait()
-        for r in range(0, ROWS, 8):
-            rows = slice(r, r + 8)
-            hc, de, dw, dn, ds_, wet = [height[j, rows] for j in range(6)]
-            for k in range(i * group, (i + 1) * group):
-                grown = (
-                    jnp.where(wet > float(k), hc, 0.0)
-                    + (faces[k, 1, rows] * de + faces[k, 2, rows] * dw)
-                    + (faces[k, 3, rows] * dn + faces[k, 4, rows] * ds_)
-                )
-                out[k, rows] = faces[k, 0, rows] + th[k] * grown
-        stores.append(pltpu.make_async_copy(out.at[p], out_h.at[p], sem.at[2 + i]))
-        stores[-1].start()
+    for load, store in zip(loads, stores):
+        load.wait()
+        store.start()
     for store in stores:
         store.wait()
 
@@ -610,8 +608,9 @@
             return pltpu.VMEM(shape, dtype)
 
         cube = (levels, ROWS, LANES)
+        group = 5 if levels % 5 == 0 else 1
         scratch = [
-            pltpu.SMEM((LANES,), jnp.int32),
+            pltpu.SMEM((levels,), f32), pltpu.SMEM((LANES,), jnp.int32),
             vmem(levels, 80, LANES), vmem(*cube), vmem(*cube), vmem(*cube),
             vmem(ROWS, LANES, dtype=jnp.int32),
             vmem(2, 96, LANES), vmem(2, 96, LANES),
@@ -622,10 +621,10 @@
             vmem(16, LANES), vmem(ngx * 16, LANES), vmem(ngx * 6, LANES),
             vmem(nz, FOLD, LANES), vmem(2, FOLD, LANES), vmem(ny, 2, FOLD, LANES),
             vmem(ROWS, LANES),
-            vmem(80, LANES), vmem(80, LANES),
-            vmem(levels, 5, ROWS, LANES), vmem(6, 96, LANES),
+            vmem(group, 80, LANES), vmem(group, 80, LANES),
+            vmem(levels, 5, ROWS, LANES), vmem(6, 96, LANES), vmem(*cube),
             vmem(1, LANES), vmem(max(8, nz * nc), LANES), vmem(1, LANES), vmem(8 if nx * ny < 8 else 32, LANES), vmem(1, LANES), vmem(16, LANES),
-            pltpu.SemaphoreType.DMA((7,)), pltpu.SemaphoreType.DMA((2,)),
+            pltpu.SemaphoreType.DMA((8,)), pltpu.SemaphoreType.DMA((levels // group,)),
             pltpu.SemaphoreType.DMA((12,)), pltpu.SemaphoreType.DMA((8,)),
             pltpu.SemaphoreType.DMA((4,)), pltpu.SemaphoreType.DMA((4,)),
             pltpu.SemaphoreType.DMA((6,)), pltpu.SemaphoreType.DMA((2,)),
@@ -633,31 +632,29 @@
         ]
         hbm = pl.BlockSpec(memory_space=pltpu.HBM)
         limit = 62 * 1024 * 1024
-        faces, height = pl.pallas_call(
-            functools.partial(kernel, nz, ny, nc, nx, levels),
-            out_shape=(
-                jax.ShapeDtypeStruct((levels, 5, ROWS, LANES), f32),
-                jax.ShapeDtypeStruct((6, ROWS, LANES), f32),
-            ),
-            in_specs=[hbm] * 7,
+        shapes = (jax.ShapeDtypeStruct(cube, f32), jax.ShapeDtypeStruct((ROWS, LANES), f32))
+        results = pl.pallas_call(
+            functools.partial(kernel, nz, ny, nc, nx, levels, group),
+            out_shape=shapes,
+            in_specs=[hbm] * 8,
             out_specs=(hbm, hbm),
             scratch_shapes=scratch,
             compiler_params=pltpu.CompilerParams(
                 collective_id=0, has_side_effects=True, vmem_limit_bytes=limit
             ),
-        )(cot, b, u, v, kap, dep, fp)
-        group = 5 if levels % 5 == 0 else 1
+        )(cot, b, u, v, kap, th, dep, fp)
+        parts = levels // group + 1
         return pl.pallas_call(
-            functools.partial(finish, levels, group),
-            out_shape=(jax.ShapeDtypeStruct(cube, f32), jax.ShapeDtypeStruct((ROWS, LANES), f32)),
-            in_specs=[hbm] * 3,
+            functools.partial(hand_on, levels, group),
+            out_shape=shapes,
+            in_specs=[hbm] * 2,
             out_specs=(hbm, hbm),
             scratch_shapes=[
-                pltpu.SMEM((levels,), f32), vmem(levels, 5, ROWS, LANES), vmem(6, ROWS, LANES), vmem(*cube),
-                pltpu.SemaphoreType.DMA((2 + levels // group,)),
+                vmem(*cube), vmem(ROWS, LANES),
+                pltpu.SemaphoreType.DMA((parts,)), pltpu.SemaphoreType.DMA((parts,)),
             ],
             compiler_params=pltpu.CompilerParams(vmem_limit_bytes=limit),
-        )(faces, height, th)
+        )(*results)
 
     in_specs = (
         P(None, "gy", "gx"), P("gy", "gx"), P(None, "gy", "gx"), P(None, "gy", "gx"),

time: 31.1 us -> 29 us (0.932); the launches traced: 30.6 us -> 28.9 us
  Pallas kernels: 29.9 us -> 28.3 us
    pallas_call x2, Pallas kernels: 29.9 us -> 28.3 us  [the longest x1 26.3 us: local(): pl.pallas_call(functools.partial(kernel, nz, ny, nc, nx, levels, group),...]
where the time goes in v4:
time: 29 us; the launch traced here: 28.9 us
  Pallas kernels  28.3 us (98%)
  between operations  0.64 us (2%)
    pallas_call x1, Pallas kernels, local(): pl.pallas_call(functools.partial(kernel, nz, ny, nc, nx, levels, group),...  26.3 us
    pallas_call x1, Pallas kernels, local(): pl.pallas_call(functools.partial(hand_on, levels, group), out_shape=shape...  2.01 us

profile of v4, /device:TPU:1, one launch (start us, length us, event | category | flops | bytes accessed | tf_op | source)
XLA Modules:
  0.0 28.9 jit_solution(8264186196899537748)
XLA Ops:
  0.6 26.3 %shard_map.95 = (f32[25,64,128]{2,1,0:T(8,128)}, f32[64,128]{1,0:T(8,128)}) custom-call(f32[25,64,128]{2,1,0:T(8,128)} %cot_h.1, f32[64,128]{1,0:T(8,128)} %b_h.1, f32[25,64,128]{2,1,0:T(8,128)} %u_h.1, f32[25,64,128]{2,1,0:T(8,128)} %v_h.1, f32[25,64,128]{2,1,0:T(8,128)} %k_h.1, f32[25]{0:T(128)} %th_h.1, s32[64,128]{1,0:T(8,128)} %dep_h.1, s32[128]{0:T(128)} %fp_h.1), custom_call_target="tpu_custom_call" | custom-call | tf_op jit(solution)/shard_map/pallas_call | solution.py:636
  26.9 2.0 %shard_map.96 = (f32[25,64,128]{2,1,0:T(8,128)}, f32[64,128]{1,0:T(8,128)}) custom-call(f32[25,64,128]{2,1,0:T(8,128)} %get-tuple-element.4.from_h, f32[64,128]{1,0:T(8,128)} %get-tuple-element.5.hfrom_h), custom_call_target="tpu_custom_call" | custom-call | tf_op jit(solution)/shard_map/pallas_call | solution.py:647

commit v5 on v4

--- a/solution.py
+++ b/solution.py
@@ -66,9 +66,9 @@
     th_s, fp_s, cot, u, v, kap, dint, plane, wide, pack2, got2, dmin, vec1, vec2,
     edge_ew, got_ew, edge_n, edge_s, got_n, got_s,
     top2, all2, mir, foldz, fold_stage, fold_y, sides,
-    qn, qs, faces, hv, outv,
+    qn, qs, faces, hv,
     mom, red1, mom2, red2, band, tot,
-    load_sem, store_sem, send_sem, halo_sem, edge_sem, red_sem, fold_sem, band_sem, ready_sem,
+    load_sem, send_sem, halo_sem, edge_sem, red_sem, fold_sem, band_sem, ready_sem,
 ):
     gx, gy = lax.axis_index("gx"), lax.axis_index("gy")
     ngx, ngy = ny * nz, nx * nc
@@ -533,12 +533,7 @@
     hv[3, inner] = hv[0, PAD + 1:PAD + 1 + ROWS] - inner_mid
     hv[4, inner] = inner_mid - hv[0, PAD - 1:PAD - 1 + ROWS]
     hv[5, inner] = plane[1, inner]
-    height = pltpu.make_async_copy(hv.at[0, inner], hadj_h, load_sem.at[0])
-    height.start()
-
-    def store_of(g):
-        part = pl.ds(g * group, group)
-        return pltpu.make_async_copy(outv.at[part], out_h.at[part], store_sem.at[g])
+    hadj_h[...] = inner_mid
 
     def finish_levels(g, carry):
         for r in range(0, ROWS, 8):
@@ -550,8 +545,7 @@
                     + (faces[k, 1, rows] * de + faces[k, 2, rows] * dw)
                     + (faces[k, 3, rows] * dn + faces[k, 4, rows] * ds_)
                 )
-                outv[k, rows] = faces[k, 0, rows] + th_s[k] * grown
-        store_of(g).start()
+                out_h[k, rows] = faces[k, 0, rows] + th_s[k] * grown
         return carry
 
     lax.fori_loop(0, levels // group, finish_levels, 0)
@@ -572,22 +566,13 @@
         pltpu.make_async_copy(foldz.at[pl.ds(0, nz - 1)], foldz.at[pl.ds(0, nz - 1)], fold_sem.at[2]).wait()
         pltpu.make_async_copy(fold_y.at[pl.ds(0, ny - 1)], fold_y.at[pl.ds(0, ny - 1)], fold_sem.at[4]).wait()
 
-    height.wait()
-    for g in range(levels // group):
-        store_of(g).wait()
-
-
-def hand_on(levels, group, from_h, hfrom_h, out_h, hout_h, held, hheld, sem_in, sem_out):
-    parts = [pl.ds(k, group) for k in range(0, levels, group)]
-    last = len(parts)
-    loads = [pltpu.make_async_copy(from_h.at[p], held.at[p], sem_in.at[i]) for i, p in enumerate(parts)]
-    loads.append(pltpu.make_async_copy(hfrom_h, hheld, sem_in.at[last]))
-    stores = [pltpu.make_async_copy(held.at[p], out_h.at[p], sem_out.at[i]) for i, p in enumerate(parts)]
-    stores.append(pltpu.make_async_copy(hheld, hout_h, sem_out.at[last]))
-    for load in loads:
-        load.start()
-    for load, store in zip(loads, stores):
-        load.wait()
+
+def hand_on(from_v, hfrom_v, out_h, hout_h, sem):
+    stores = [
+        pltpu.make_async_copy(from_v, out_h, sem.at[0]),
+        pltpu.make_async_copy(hfrom_v, hout_h, sem.at[1]),
+    ]
+    for store in stores:
         store.start()
     for store in stores:
         store.wait()
@@ -622,37 +607,35 @@
             vmem(nz, FOLD, LANES), vmem(2, FOLD, LANES), vmem(ny, 2, FOLD, LANES),
             vmem(ROWS, LANES),
             vmem(group, 80, LANES), vmem(group, 80, LANES),
-            vmem(levels, 5, ROWS, LANES), vmem(6, 96, LANES), vmem(*cube),
+            vmem(levels, 5, ROWS, LANES), vmem(6, 96, LANES),
             vmem(1, LANES), vmem(max(8, nz * nc), LANES), vmem(1, LANES), vmem(8 if nx * ny < 8 else 32, LANES), vmem(1, LANES), vmem(16, LANES),
-            pltpu.SemaphoreType.DMA((8,)), pltpu.SemaphoreType.DMA((levels // group,)),
+            pltpu.SemaphoreType.DMA((8,)),
             pltpu.SemaphoreType.DMA((12,)), pltpu.SemaphoreType.DMA((8,)),
             pltpu.SemaphoreType.DMA((4,)), pltpu.SemaphoreType.DMA((4,)),
             pltpu.SemaphoreType.DMA((6,)), pltpu.SemaphoreType.DMA((2,)),
             pltpu.SemaphoreType.REGULAR,
         ]
         hbm = pl.BlockSpec(memory_space=pltpu.HBM)
-        limit = 62 * 1024 * 1024
+        limit = 48 * 1024 * 1024
         shapes = (jax.ShapeDtypeStruct(cube, f32), jax.ShapeDtypeStruct((ROWS, LANES), f32))
+        inputs = [pltpu.with_memory_space_constraint(a, pltpu.HBM) for a in (cot, b, u, v, kap, th, dep, fp)]
+        held = pl.BlockSpec(memory_space=pltpu.VMEM)
         results = pl.pallas_call(
             functools.partial(kernel, nz, ny, nc, nx, levels, group),
             out_shape=shapes,
             in_specs=[hbm] * 8,
-            out_specs=(hbm, hbm),
+            out_specs=(held, held),
             scratch_shapes=scratch,
             compiler_params=pltpu.CompilerParams(
                 collective_id=0, has_side_effects=True, vmem_limit_bytes=limit
             ),
-        )(cot, b, u, v, kap, th, dep, fp)
-        parts = levels // group + 1
+        )(*inputs)
         return pl.pallas_call(
-            functools.partial(hand_on, levels, group),
+            hand_on,
             out_shape=shapes,
-            in_specs=[hbm] * 2,
+            in_specs=[held, held],
             out_specs=(hbm, hbm),
-            scratch_shapes=[
-                vmem(*cube), vmem(ROWS, LANES),
-                pltpu.SemaphoreType.DMA((parts,)), pltpu.SemaphoreType.DMA((parts,)),
-            ],
+            scratch_shapes=[pltpu.SemaphoreType.DMA((2,))],
             compiler_params=pltpu.CompilerParams(vmem_limit_bytes=limit),
         )(*results)
 

time: 29 us -> 27.2 us (0.938)
  Pallas kernels: 28.3 us -> 26.5 us
    pallas_call x1, Pallas kernels: 2.01 us -> 0.91 us  [local(): pl.pallas_call(hand_on, out_shape=shapes, in_specs=[held, held], out_spec...]
    pallas_call x1, Pallas kernels: 26.3 us -> 25.6 us  [local(): pl.pallas_call(functools.partial(kernel, nz, ny, nc, nx, levels, group),...]
where the time goes in v5:
time: 27.2 us; the launch traced here: 27.1 us
  Pallas kernels  26.5 us (97%)
  between operations  0.64 us (2%)
    pallas_call x1, Pallas kernels, local(): pl.pallas_call(functools.partial(kernel, nz, ny, nc, nx, levels, group),...  25.6 us
    pallas_call x1, Pallas kernels, local(): pl.pallas_call(hand_on, out_shape=shapes, in_specs=[held, held], out_spec...  0.91 us

profile of v5, /device:TPU:1, one launch (start us, length us, event | category | flops | bytes accessed | tf_op | source)
XLA Modules:
  0.0 27.1 jit_solution(8830506344967739238)
XLA Ops:
  0.6 25.6 %shard_map.95 = (f32[25,64,128]{2,1,0:T(8,128)S(1)}, f32[64,128]{1,0:T(8,128)S(1)}) custom-call(f32[25,64,128]{2,1,0:T(8,128)} %cot_h.1, f32[64,128]{1,0:T(8,128)} %b_h.1, f32[25,64,128]{2,1,0:T(8,128)} %u_h.1, f32[25,64,128]{2,1,0:T(8,128)} %v_h.1, f32[25,64,128]{2,1,0:T(8,128)} %k_h.1, f32[25]{0:T(128)} %th_h.1, s32[64,128]{1,0:T(8,128)} %dep_h.1, s32[128]{0:T(128)} %fp_h.1), custom_call_target="tpu_custom_call" | custom-call | tf_op jit(solution)/shard_map/pallas_call | solution.py:623
  26.2 0.9 %shard_map.96 = (f32[25,64,128]{2,1,0:T(8,128)}, f32[64,128]{1,0:T(8,128)}) custom-call(f32[25,64,128]{2,1,0:T(8,128)S(1)} %get-tuple-element.4.from_v, f32[64,128]{1,0:T(8,128)S(1)} %get-tuple-element.5.hfrom_v), custom_call_target="tpu_custom_call" | custom-call | tf_op jit(solution)/shard_map/pallas_call | solution.py:633

commit v6 on v5

--- a/solution.py
+++ b/solution.py
@@ -62,11 +62,11 @@
 
 def kernel(
     nz, ny, nc, nx, levels, group,
-    cot_h, b_h, u_h, v_h, k_h, th_h, dep_h, fp_h, out_h, hadj_h,
+    cot_h, b_h, u_h, v_h, k_h, th_h, dep_h, fp_h, faces, hv,
     th_s, fp_s, cot, u, v, kap, dint, plane, wide, pack2, got2, dmin, vec1, vec2,
     edge_ew, got_ew, edge_n, edge_s, got_n, got_s,
     top2, all2, mir, foldz, fold_stage, fold_y, sides,
-    qn, qs, faces, hv,
+    qn, qs, tall,
     mom, red1, mom2, red2, band, tot,
     load_sem, send_sem, halo_sem, edge_sem, red_sem, fold_sem, band_sem, ready_sem,
 ):
@@ -93,7 +93,7 @@
         pltpu.make_async_copy(fp_h, fp_s, load_sem.at[6]),
         pltpu.make_async_copy(th_h, th_s, load_sem.at[7]),
     ]
-    for load in loads:
+    for load in loads[:2]:
         load.start()
 
     barrier = pltpu.get_barrier_semaphore()
@@ -138,6 +138,9 @@
         greet(at(*d))
     group1(greet)
     group2(greet)
+
+    for load in loads[2:]:
+        load.start()
 
     zero8 = jnp.zeros((8, LANES), f32)
     for part, n in ((red1, n1), (red2, n2 + 1)):
@@ -151,9 +154,17 @@
     loads[1].wait()
     depth_f = dint[...].astype(f32)
     plane[1, PAD:PAD + ROWS] = depth_f
-    pack2[...] = jnp.where(
-        (lane < 32) | (lane >= 96), plane[0, PAD:PAD + ROWS], roll_lanes(depth_f, 64)
-    )
+    lane16 = lax.broadcasted_iota(jnp.int32, (16, LANES), 1)
+    packed = jnp.zeros((16, LANES), f32)
+    for i in range(4):
+        some = slice(PAD + 16 * i, PAD + 16 * i + 16)
+        part = jnp.where(
+            (lane16 & 31) < 20,
+            roll_lanes(plane[0, some], 16 + 32 * i),
+            roll_lanes(plane[1, some], (24 + 32 * i) % LANES),
+        )
+        packed = jnp.where(lane16 >> 5 == i, part, packed)
+    pack2[...] = packed
 
     pl.semaphore_wait(barrier, 8 + n1 - 1 + n2 - 1)
 
@@ -174,11 +185,11 @@
         else:
             side = 0 if dx == 1 else 1
             if dy == 0:
-                src, dst = pack2, got2.at[side, pl.ds(8, ROWS)]
+                src, dst = pack2, got2.at[side, pl.ds(8, 16)]
             elif dy == 1:
-                src, dst = pack2.at[pl.ds(ROWS - 8, 8)], got2.at[side, pl.ds(0, 8)]
+                src, dst = pack2.at[pl.ds(8, 8)], got2.at[side, pl.ds(0, 8)]
             else:
-                src, dst = pack2.at[pl.ds(0, 8)], got2.at[side, pl.ds(ROWS + 8, 8)]
+                src, dst = pack2.at[pl.ds(0, 8)], got2.at[side, pl.ds(24, 8)]
         halos.append(send(src, dst, send_sem.at[i], halo_sem.at[i], at(dx, dy)))
 
     for halo in halos:
@@ -241,9 +252,12 @@
 
     for halo in halos:
         halo.wait_recv()
-    hw, he = got2[0], got2[1]
-    wide[0, 8:88] = jnp.where(lane80 < 64, he, hw)
-    wide[1, 8:88] = roll_lanes(jnp.where(lane80 < 64, hw, he), 64)
+    for rows, to, i in [((0, 8), 8, 3), *(((8, 24), PAD + 16 * i, i) for i in range(4)), ((24, 32), PAD + ROWS, 0)]:
+        west, east = got2[0, slice(*rows)], got2[1, slice(*rows)]
+        spot = lane16[:rows[1] - rows[0]] & 31
+        there = slice(to, to + rows[1] - rows[0])
+        wide[0, there] = roll_lanes(jnp.where(spot < 16, west, east), (LANES - 16 - 32 * i) % LANES)
+        wide[1, there] = roll_lanes(jnp.where(spot < 24, west, east), (LANES - 24 - 32 * i) % LANES)
 
     loads[6].wait()
     seam = fp_s[0] + gx * LANES + 1
@@ -331,7 +345,6 @@
         edge.wait_recv()
 
     sides[...] = jnp.where((lane & 1) == 1, got_ew[1], got_ew[0])
-    lane16 = lax.broadcasted_iota(jnp.int32, (16, LANES), 1)
 
     def level_group(begin, end, g, carry):
         ks = [g * group + j for j in range(group)]
@@ -364,11 +377,14 @@
                 kw = jnp.where(dmin[1, 0, mid] > kf, time_step * (qw + q_w), 0.0)
                 kn = jnp.where(dmin[2, 0, mid] > kf, time_step * (qn[j, mid] + qn[j, 9 + r:25 + r]), 0.0)
                 ks_ = jnp.where(dmin[3, 0, mid] > kf, time_step * (qs[j, mid] + qs[j, 7 + r:23 + r]), 0.0)
+                heavy = th_s[k]
                 for i, face in enumerate((ke, kw, kn, ks_)):
-                    faces[k, 1 + i, rows] = face
+                    faces[k, 1 + i, rows] = heavy * face
+                faces[k, 5, rows] = jnp.where(plane[1, PAD + r:PAD + r + 16] > kf, heavy, 0.0)
                 faces[k, 0, rows] = ct + (ke * (c_e - ct) + kw * (ct - c_w)) + (kn * (c_n - ct) + ks_ * (ct - c_s))
         return carry
 
+    loads[7].wait()
     cut = 48
     lax.fori_loop(0, levels // group, functools.partial(level_group, 0, cut), 0)
 
@@ -469,8 +485,6 @@
         got_n[...] = jnp.where(row < levels, got, -got)
 
     lax.fori_loop(0, levels // group, functools.partial(level_group, cut, ROWS), 0)
-    loads[7].wait()
-
     wait_red(red2, n2, red_sem.at[3])
 
     @pl.when(gy != ngy - 1)
@@ -525,30 +539,14 @@
     rows80 = [spread(a, 80) for a in (a0, a1, y2)]
     h_mid = rows80[0] * plane[0, body] + rows80[1] * vec1[0, body] + rows80[2] * vec2[0, body]
     h_side = rows80[0] * wide[0, body] + rows80[1] * vec1[1, body] + rows80[2] * vec2[1, body]
-    hv[0, body] = h_mid
+    tall[body] = h_mid
     inner_mid, inner_side = h_mid[8:8 + ROWS], h_side[8:8 + ROWS]
     h_e, h_w = neighbours(inner_mid, inner_side, ROWS)
-    hv[1, inner] = h_e - inner_mid
-    hv[2, inner] = inner_mid - h_w
-    hv[3, inner] = hv[0, PAD + 1:PAD + 1 + ROWS] - inner_mid
-    hv[4, inner] = inner_mid - hv[0, PAD - 1:PAD - 1 + ROWS]
-    hv[5, inner] = plane[1, inner]
-    hadj_h[...] = inner_mid
-
-    def finish_levels(g, carry):
-        for r in range(0, ROWS, 8):
-            rows = slice(r, r + 8)
-            hc, de, dw, dn, ds_, wet = [hv[i, PAD + r:PAD + r + 8] for i in range(6)]
-            for k in [g * group + j for j in range(group)]:
-                grown = (
-                    jnp.where(wet > k.astype(f32), hc, 0.0)
-                    + (faces[k, 1, rows] * de + faces[k, 2, rows] * dw)
-                    + (faces[k, 3, rows] * dn + faces[k, 4, rows] * ds_)
-                )
-                out_h[k, rows] = faces[k, 0, rows] + th_s[k] * grown
-        return carry
-
-    lax.fori_loop(0, levels // group, finish_levels, 0)
+    hv[0] = inner_mid
+    hv[1] = h_e - inner_mid
+    hv[2] = inner_mid - h_w
+    hv[3] = tall[PAD + 1:PAD + 1 + ROWS] - inner_mid
+    hv[4] = inner_mid - tall[PAD - 1:PAD - 1 + ROWS]
 
     for halo in halos:
         halo.wait_send()
@@ -567,13 +565,22 @@
         pltpu.make_async_copy(fold_y.at[pl.ds(0, ny - 1)], fold_y.at[pl.ds(0, ny - 1)], fold_sem.at[4]).wait()
 
 
-def hand_on(from_v, hfrom_v, out_h, hout_h, sem):
-    stores = [
-        pltpu.make_async_copy(from_v, out_h, sem.at[0]),
-        pltpu.make_async_copy(hfrom_v, hout_h, sem.at[1]),
-    ]
-    for store in stores:
-        store.start()
+def finish(levels, group, faces, hv, out_h, hadj_h, out, sem):
+    stores = [pltpu.make_async_copy(hv.at[0], hadj_h, sem.at[0])]
+    stores[0].start()
+    for g in range(levels // group):
+        for r in range(0, ROWS, 8):
+            rows = slice(r, r + 8)
+            hc, de, dw, dn, ds_ = [hv[i, rows] for i in range(5)]
+            for k in range(g * group, (g + 1) * group):
+                out[k, rows] = (
+                    (faces[k, 0, rows] + faces[k, 5, rows] * hc)
+                    + (faces[k, 1, rows] * de + faces[k, 2, rows] * dw)
+                    + (faces[k, 3, rows] * dn + faces[k, 4, rows] * ds_)
+                )
+        part = pl.ds(g * group, group)
+        stores.append(pltpu.make_async_copy(out.at[part], out_h.at[part], sem.at[1 + g]))
+        stores[-1].start()
     for store in stores:
         store.wait()
 
@@ -599,7 +606,7 @@
             vmem(levels, 80, LANES), vmem(*cube), vmem(*cube), vmem(*cube),
             vmem(ROWS, LANES, dtype=jnp.int32),
             vmem(2, 96, LANES), vmem(2, 96, LANES),
-            vmem(ROWS, LANES), vmem(2, 80, LANES), vmem(4, 2, 80, LANES),
+            vmem(16, LANES), vmem(2, 32, LANES), vmem(4, 2, 80, LANES),
             vmem(2, 96, LANES), vmem(2, 96, LANES),
             vmem(ROWS, LANES), vmem(2, ROWS, LANES),
             vmem(FOLD, LANES), vmem(FOLD, LANES), vmem(FOLD, LANES), vmem(FOLD, LANES),
@@ -607,7 +614,7 @@
             vmem(nz, FOLD, LANES), vmem(2, FOLD, LANES), vmem(ny, 2, FOLD, LANES),
             vmem(ROWS, LANES),
             vmem(group, 80, LANES), vmem(group, 80, LANES),
-            vmem(levels, 5, ROWS, LANES), vmem(6, 96, LANES),
+            vmem(96, LANES),
             vmem(1, LANES), vmem(max(8, nz * nc), LANES), vmem(1, LANES), vmem(8 if nx * ny < 8 else 32, LANES), vmem(1, LANES), vmem(16, LANES),
             pltpu.SemaphoreType.DMA((8,)),
             pltpu.SemaphoreType.DMA((12,)), pltpu.SemaphoreType.DMA((8,)),
@@ -622,7 +629,10 @@
         held = pl.BlockSpec(memory_space=pltpu.VMEM)
         results = pl.pallas_call(
             functools.partial(kernel, nz, ny, nc, nx, levels, group),
-            out_shape=shapes,
+            out_shape=(
+                jax.ShapeDtypeStruct((levels, 6, ROWS, LANES), f32),
+                jax.ShapeDtypeStruct((5, ROWS, LANES), f32),
+            ),
             in_specs=[hbm] * 8,
             out_specs=(held, held),
             scratch_shapes=scratch,
@@ -631,11 +641,11 @@
             ),
         )(*inputs)
         return pl.pallas_call(
-            hand_on,
+            functools.partial(finish, levels, group),
             out_shape=shapes,
             in_specs=[held, held],
             out_specs=(hbm, hbm),
-            scratch_shapes=[pltpu.SemaphoreType.DMA((2,))],
+            scratch_shapes=[vmem(*cube), pltpu.SemaphoreType.DMA((1 + levels // group,))],
             compiler_params=pltpu.CompilerParams(vmem_limit_bytes=limit),
         )(*results)
 

time: 27.2 us -> 26.8 us (0.985)
  Pallas kernels: 26.5 us -> 26 us
    pallas_call x1, Pallas kernels: 25.6 us -> 24.9 us  [local(): pl.pallas_call(functools.partial(kernel, nz, ny, nc, nx, levels, group),...]
where the time goes in v6:
time: 26.8 us; the launch traced here: 26.7 us
  Pallas kernels  26 us (97%)
  between operations  0.64 us (2%)
    pallas_call x1, Pallas kernels, local(): pl.pallas_call(functools.partial(kernel, nz, ny, nc, nx, levels, group),...  24.9 us
    pallas_call x1, Pallas kernels, local(): pl.pallas_call(functools.partial(finish, levels, group), out_shape=shapes...  1.07 us

profile of v6, /device:TPU:1, one launch (start us, length us, event | category | flops | bytes accessed | tf_op | source)
XLA Modules:
  0.0 26.7 jit_solution(3448977559435608653)
XLA Ops:
  0.6 24.9 %shard_map.95 = (f32[25,6,64,128]{3,2,1,0:T(8,128)S(1)}, f32[5,64,128]{2,1,0:T(8,128)S(1)}) custom-call(f32[25,64,128]{2,1,0:T(8,128)} %cot_h.1, f32[64,128]{1,0:T(8,128)} %b_h.1, f32[25,64,128]{2,1,0:T(8,128)} %u_h.1, f32[25,64,128]{2,1,0:T(8,128)} %v_h.1, f32[25,64,128]{2,1,0:T(8,128)} %k_h.1, f32[25]{0:T(128)} %th_h.1, s32[64,128]{1,0:T(8,128)} %dep_h.1, ...), custom_call_target="tpu_custom_call" | custom-call | tf_op jit(solution)/shard_map/pallas_call | solution.py:630
  25.6 1.1 %shard_map.96 = (f32[25,64,128]{2,1,0:T(8,128)}, f32[64,128]{1,0:T(8,128)}) custom-call(f32[25,6,64,128]{3,2,1,0:T(8,128)S(1)} %get-tuple-element.4.faces, f32[5,64,128]{2,1,0:T(8,128)S(1)} %get-tuple-element.5.hv), custom_call_target="tpu_custom_call" | custom-call | tf_op jit(solution)/shard_map/pallas_call | solution.py:643

commit v7 on v6

--- a/solution.py
+++ b/solution.py
@@ -127,6 +127,8 @@
             if (d, e) != (0, 0):
                 act(((y + d) % ny * nz + z, (x + e) % nx * nc + c))
 
+    group1, group2, n1, n2, me1, me2 = group2, group1, n2, n1, me2, me1
+
     def everyone_on_top(act):
         for pz in far_z[:-1]:
             for py in far_y:
@@ -134,10 +136,10 @@
         for py in far_y[:-1]:
             act((py + z, gy))
 
+    group1(greet)
+    group2(greet)
     for d in compass:
         greet(at(*d))
-    group1(greet)
-    group2(greet)
 
     for load in loads[2:]:
         load.start()

time: 26.8 us -> 26.7 us (level)
  no operation moved by 1% of the time
where the time goes in v7:
time: 26.7 us; the launch traced here: 26.5 us
  Pallas kernels  25.9 us (97%)
  between operations  0.64 us (2%)
    pallas_call x1, Pallas kernels, local(): pl.pallas_call(functools.partial(kernel, nz, ny, nc, nx, levels, group),...  24.8 us
    pallas_call x1, Pallas kernels, local(): pl.pallas_call(functools.partial(finish, levels, group), out_shape=shapes...  1.07 us

profile of v7, /device:TPU:1, one launch (start us, length us, event | category | flops | bytes accessed | tf_op | source)
XLA Modules:
  0.0 26.5 jit_solution(2471511501239103311)
XLA Ops:
  0.6 24.8 %shard_map.95 = (f32[25,6,64,128]{3,2,1,0:T(8,128)S(1)}, f32[5,64,128]{2,1,0:T(8,128)S(1)}) custom-call(f32[25,64,128]{2,1,0:T(8,128)} %cot_h.1, f32[64,128]{1,0:T(8,128)} %b_h.1, f32[25,64,128]{2,1,0:T(8,128)} %u_h.1, f32[25,64,128]{2,1,0:T(8,128)} %v_h.1, f32[25,64,128]{2,1,0:T(8,128)} %k_h.1, f32[25]{0:T(128)} %th_h.1, s32[64,128]{1,0:T(8,128)} %dep_h.1, ...), custom_call_target="tpu_custom_call" | custom-call | tf_op jit(solution)/shard_map/pallas_call | solution.py:632
  25.5 1.1 %shard_map.96 = (f32[25,64,128]{2,1,0:T(8,128)}, f32[64,128]{1,0:T(8,128)}) custom-call(f32[25,6,64,128]{3,2,1,0:T(8,128)S(1)} %get-tuple-element.4.faces, f32[5,64,128]{2,1,0:T(8,128)S(1)} %get-tuple-element.5.hv), custom_call_target="tpu_custom_call" | custom-call | tf_op jit(solution)/shard_map/pallas_call | solution.py:645
